TPU v7x, 512 devices: a whole 4x8x8 slice. The times are simulated.
512 devices in a mesh: grp: 16 (over y, z_lo), row: 32 (over z_hi, x, core).
Axes of the slice: x: 4, y: 8, z: 8 (z_hi: 4, z_lo: 2; z = z_hi * 2 + z_lo), core: 2. Of those that a mesh axis runs over, the one named last changes fastest.
Arguments:
- cov_prior: float32 [16384, 16384], P(('grp', 'row')), may hold values from -7 to 23, as said below
- courant_x_field: float32 [128, 128], replicated, may hold values from -0.35 to 0.35
- courant_y_field: float32 [128, 128], replicated, may hold values from -0.35 to 0.35
- obs_cells: int32 [2, 128], replicated, may hold values from 0 to 16383
- obs_var: float32 [2, 128], replicated, may hold values from 0.5 to 2
Outputs:
- analysis: float32 [16384, 16384], P('grp', 'row')
Inputs may be any that keep to these rules, and one draw needn't show every extreme that they name: `cov_prior`: symmetric and positive definite. `obs_cells`: a cell may be observed more than once in an update.
All inputs are finite; a program needn't handle non-finite values.
Results may differ from a plain program's by a relative error of at most 0.0002.
Values sent between devices are 32-bit elements; how exact they have to be, the bound alone decides.
A program may use at most 64 MiB of HBM per device.

v0:
```python
import jax
import jax.numpy as jnp
from jax import lax
from jax.sharding import PartitionSpec as P

ZONAL_POINTS = 128
NY = 128
NCELL = 16384
UPDATES = 2


diffusion = 0.1


def extended_2(block, sides, width):
    for axis, dim in sides:
        count = lax.axis_size(axis)
        forward = [(i, i + 1) for i in range(count - 1)]
        backward = [(target, source) for source, target in forward]
        low = lax.ppermute(
            lax.slice_in_dim(block, block.shape[dim] - width, None, axis=dim), axis, forward
        )
        high = lax.ppermute(lax.slice_in_dim(block, 0, width, axis=dim), axis, backward)
        block = jnp.concatenate([low, block, high], axis=dim)
    return block


def tendency_first(padded, u_part, v_part):
    middle = padded[:, 2:-2]
    center = middle[:, :, 2:-2]
    along_x = (
        8.0 * (middle[:, :, 3:-1] - middle[:, :, 1:-3]) - (middle[:, :, 4:] - middle[:, :, :-4])
    ) / 12.0
    column = padded[:, :, 2:-2]
    along_y = (8.0 * (column[:, 3:-1] - column[:, 1:-3]) - (column[:, 4:] - column[:, :-4])) / 12.0
    laplace = (
        middle[:, :, 3:-1] + middle[:, :, 1:-3] + column[:, 3:-1] + column[:, 1:-3] - 4.0 * center
    )
    return diffusion * laplace - u_part * along_x - v_part * along_y


def heun_whole(fields, courant_x_field, courant_y_field):
    slope_first = tendency_first(
        jnp.pad(fields, ((0, 0), (2, 2), (2, 2))), courant_x_field, courant_y_field
    )
    latter_increment = tendency_first(
        jnp.pad(fields + slope_first, ((0, 0), (2, 2), (2, 2))), courant_x_field, courant_y_field
    )
    return fields + 0.5 * (slope_first + latter_increment)


def tendency_last(extended, u_part, v_part):
    padded = jnp.pad(extended, ((0, 0), (2, 2), (0, 0)))
    middle = padded[2:-2]
    center = middle[:, 2:-2]
    along_x = (8.0 * (middle[:, 3:-1] - middle[:, 1:-3]) - (middle[:, 4:] - middle[:, :-4])) / 12.0
    column = padded[:, 2:-2]
    along_y = (8.0 * (column[3:-1] - column[1:-3]) - (column[4:] - column[:-4])) / 12.0
    laplace = middle[:, 3:-1] + middle[:, 1:-3] + column[3:-1] + column[1:-3] - 4.0 * center
    return diffusion * laplace - u_part * along_x - v_part * along_y


def linear_source_term(local_block, courant_x_field, courant_y_field):
    meridional_count = local_block.shape[0]
    first_row = lax.axis_index("grp") * meridional_count
    u_padded = jnp.pad(courant_x_field, ((4, 4), (0, 0)))
    v_padded = jnp.pad(courant_y_field, ((4, 4), (0, 0)))
    u_inner = lax.dynamic_slice_in_dim(u_padded, first_row + 4, meridional_count, 0)[:, :, None]
    v_inner = lax.dynamic_slice_in_dim(v_padded, first_row + 4, meridional_count, 0)[:, :, None]

    def section_slope(current):
        extended = extended_2(current, (("grp", 0),), 2)
        return tendency_last(extended, u_inner, v_inner)

    slope_first = section_slope(local_block)
    latter_increment = section_slope(local_block + slope_first)
    local_block = local_block + 0.5 * (slope_first + latter_increment)
    return local_block


def local(cov_prior, courant_x_field, courant_y_field, obs_cells, obs_var):
    row_count = cov_prior.shape[0]
    fields = cov_prior.reshape(row_count, NY, ZONAL_POINTS)
    fields = heun_whole(fields, courant_x_field, courant_y_field)
    advanced = fields.reshape(row_count, NCELL)
    members = lax.axis_size("row")
    zonal_extent = NCELL // members
    meridional_count = row_count * members // ZONAL_POINTS
    arrived_value = lax.all_to_all(advanced, "row", split_axis=1, concat_axis=0, tiled=True)
    predicted_tracer = linear_source_term(
        arrived_value.reshape(meridional_count, ZONAL_POINTS, zonal_extent),
        courant_x_field,
        courant_y_field,
    )
    posterior_mean = predicted_tracer.reshape(meridional_count * ZONAL_POINTS, zonal_extent)
    local_rows = posterior_mean.shape[0]
    first_cell = lax.axis_index("grp") * local_rows
    first_column = lax.axis_index("row") * zonal_extent
    for update_number in range(UPDATES):
        picked = obs_cells[update_number]
        row_offset = picked - first_cell
        row_owned = (row_offset >= 0) & (row_offset < local_rows)
        rows_part = jnp.where(
            row_owned[:, None], posterior_mean[jnp.clip(row_offset, 0, local_rows - 1)], 0.0
        )
        observed_rows = lax.psum(rows_part, "grp")
        column_offset = picked - first_column
        column_owned = (column_offset >= 0) & (column_offset < zonal_extent)
        safe_column = jnp.clip(column_offset, 0, zonal_extent - 1)
        cols_part = jnp.where(column_owned[None, :], posterior_mean[:, safe_column], 0.0)
        inner_part = jnp.where(column_owned[None, :], observed_rows[:, safe_column], 0.0)
        observed_cols, inner_block = lax.psum((cols_part, inner_part), "row")
        system = 0.5 * (inner_block + inner_block.T) + jnp.diag(obs_var[update_number])
        factor = jnp.linalg.cholesky(system)
        halfway = lax.linalg.triangular_solve(factor, observed_rows, left_side=True, lower=True)
        weights = lax.linalg.triangular_solve(
            factor, halfway, left_side=True, lower=True, transpose_a=True
        )
        posterior_mean = posterior_mean - jnp.dot(
            observed_cols, weights, precision=lax.Precision.HIGHEST
        )
    return posterior_mean


def solution(mesh):
    placed = (P(("grp", "row"), None), P(), P(), P(), P())
    return jax.shard_map(
        local, mesh=mesh, in_specs=placed, out_specs=P("grp", "row"), check_vma=False
    )
```

profile of v0, /device:TPU:8, one launch (start us, length us, event | category | flops | bytes accessed | tf_op | source)
XLA Modules:
  0.0 1064.2 jit_solution(17766533963469429662)
XLA Ops:
  6.5 2.0 copy.29
  8.6 2.6 bitcast_add_fusion.4
  11.2 4.0 fusion.20
  18.1 54.5 %all_to_all.16 = f32[32,32,512]{2,0,1:T(8,128)S(1)} all-to-all(f32[32,32,512]{2,0,1:T(8,128)S(1)} %copy.6), channel_id=1, replica_groups=mesh['grp'=16,'row'=32] {'row'}, dimensions={1} | all-to-all | bytes 4194304 | tf_op jit(solution)/shard_map/all_to_all | solution.py:89
  73.6 14.2 %collective-permute-start = (f32[2,128,512]{2,1,0:T(8,128)}, f32[2,128,512]{2,1,0:T(8,128)S(1)}, u32[]{:S(2)}, u32[]{:S(2)}) collective-permute-start(f32[2,128,512]{2,1,0:T(8,128)} %bitcast.2), channel_id=1, source_target_pairs={{0,32},{32,64},{64,96},{96,128},{128,160},{160,192},{192,224},{224... | collective-permute-start | bytes 1572872 | tf_op jit(solution)/shard_map/ppermute | solution.py:20
  89.8 20.8 %collective-permute-done = f32[2,128,512]{2,1,0:T(8,128)S(1)} collective-permute-done((f32[2,128,512]{2,1,0:T(8,128)}, f32[2,128,512]{2,1,0:T(8,128)S(1)}, u32[]{:S(2)}, u32[]{:S(2)}) %collective-permute-start) | collective-permute-done | bytes 524320 | tf_op jit(solution)/shard_map/ppermute | solution.py:20
  113.6 3.8 collective-permute-start.2
  117.4 3.0 collective-permute-start.3
  120.4 18.5 %collective-permute-done.2 = f32[2,128,512]{2,1,0:T(8,128)S(1)} collective-permute-done((f32[2,128,512]{2,1,0:T(8,128)S(1)}, f32[2,128,512]{2,1,0:T(8,128)S(1)}, u32[]{:S(2)}, u32[]{:S(2)}) %collective-permute-start.2) | collective-permute-done | bytes 524320 | tf_op jit(solution)/shard_map/ppermute | solution.py:20
  138.9 2.5 collective-permute-done.3
  142.1 2.9 fusion.30
  145.0 2.6 gather_fusion.1
  150.3 2.6 gather_fusion
  153.9 131.3 %all-reduce.13.cloned.1.call-done = f32[128,512]{1,0:T(8,128)} async-done(((f32[128,512]{1,0:T(8,128)}), f32[128,512]{1,0:T(8,128)}) %all-reduce.13.cloned.1.call-update) | async-done | bytes 262160 | tf_op jit(solution)/shard_map/psum | solution.py:106
  288.1 284.4 %all-reduce.19.cloned.1.call-done = (f32[1024,128]{0,1:T(8,128)}, f32[128,128]{0,1:T(8,128)}) async-done(((f32[1024,128]{0,1:T(8,128)}, f32[128,128]{0,1:T(8,128)}), (f32[1024,128]{0,1:T(8,128)}, f32[128,128]{0,1:T(8,128)})) %all-reduce.19.cloned.1.call-update) | async-done | bytes 589840 | tf_op jit(solution)/shard_map/psum | solution.py:112
  574.6 11.7 %cholesky.44 = f32[128,128]{1,0:T(8,128)S(1)} custom-call(f32[128,128]{1,0:T(8,128)S(1)} %copy.13), custom_call_target="Cholesky" | custom-call | tf_op jit(solution)/shard_map/jit(cholesky)/cholesky | solution.py:114
  587.6 9.8 custom-call.11
  598.2 3.4 convolution_subtract_fusion.1
  605.3 2.6 gather_fusion.3
  608.9 132.8 %all-reduce.15.cloned.1.call-done = f32[128,512]{1,0:T(8,128)} async-done(((f32[128,512]{1,0:T(8,128)}), f32[128,512]{1,0:T(8,128)}) %all-reduce.15.cloned.1.call-update) | async-done | bytes 262160 | tf_op jit(solution)/shard_map/psum | solution.py:106
  744.3 284.4 %all-reduce.17.cloned.1.call-done = (f32[1024,128]{0,1:T(8,128)}, f32[128,128]{1,0:T(8,128)}) async-done(((f32[1024,128]{0,1:T(8,128)}, f32[128,128]{1,0:T(8,128)}), (f32[1024,128]{0,1:T(8,128)}, f32[128,128]{1,0:T(8,128)})) %all-reduce.17.cloned.1.call-update) | async-done | bytes 589840 | tf_op jit(solution)/shard_map/psum | solution.py:112
  1030.8 11.7 %cholesky.55 = f32[128,128]{1,0:T(8,128)S(1)} custom-call(f32[128,128]{1,0:T(8,128)S(1)} %fusion.47), custom_call_target="Cholesky" | custom-call | tf_op jit(solution)/shard_map/jit(cholesky)/cholesky | solution.py:114
  1043.9 9.8 custom-call.13
  1054.5 3.2 convolution_subtract_fusion
  (81 shorter events, 31.5 us)
Async XLA Ops:
  6.5 278.7 %all-reduce.13.cloned.1.call-start = ((), (), s32[]{:S(2)}) async-start(), calls=%async_computation.1 | async-start | bytes 524288 | tf_op jit(solution)/shard_map/psum | solution.py:106
  6.5 2.0 copy-start.5
  6.5 2.0 copy-start.6
  73.6 37.0 %collective-permute-start = (f32[2,128,512]{2,1,0:T(8,128)}, f32[2,128,512]{2,1,0:T(8,128)S(1)}, u32[]{:S(2)}, u32[]{:S(2)}) collective-permute-start(f32[2,128,512]{2,1,0:T(8,128)} %bitcast.2), channel_id=1, source_target_pairs={{0,32},{32,64},{64,96},{96,128},{128,160},{160,192},{192,224},{224... | collective-permute-start | bytes 1572872 | tf_op jit(solution)/shard_map/ppermute | solution.py:20
  87.8 23.3 %collective-permute-start.1 = (f32[2,128,512]{2,1,0:T(8,128)}, f32[2,128,512]{2,1,0:T(8,128)S(1)}, u32[]{:S(2)}, u32[]{:S(2)}) collective-permute-start(f32[2,128,512]{2,1,0:T(8,128)} %bitcast.4), channel_id=1, source_target_pairs={{32,0},{64,32},{96,64},{128,96},{160,128},{192,160},{224,192},{256... | collective-permute-start | bytes 1572872 | tf_op jit(solution)/shard_map/ppermute | solution.py:23
  113.5 6.8 copy-start.7
  113.6 25.3 %collective-permute-start.2 = (f32[2,128,512]{2,1,0:T(8,128)S(1)}, f32[2,128,512]{2,1,0:T(8,128)S(1)}, u32[]{:S(2)}, u32[]{:S(2)}) collective-permute-start(f32[2,128,512]{2,1,0:T(8,128)S(1)} %get-tuple-element.17), channel_id=1, source_target_pairs={{0,32},{32,64},{64,96},{96,128},{128,160},{160,192},{192,224},{224... | collective-permute-start | bytes 1572872 | tf_op jit(solution)/shard_map/ppermute | solution.py:20
  117.4 24.1 %collective-permute-start.3 = (f32[2,128,512]{2,1,0:T(8,128)S(1)}, f32[2,128,512]{2,1,0:T(8,128)S(1)}, u32[]{:S(2)}, u32[]{:S(2)}) collective-permute-start(f32[2,128,512]{2,1,0:T(8,128)S(1)} %get-tuple-element.16), channel_id=1, source_target_pairs={{32,0},{64,32},{96,64},{128,96},{160,128},{192,160},{224,192},{256... | collective-permute-start | bytes 1572872 | tf_op jit(solution)/shard_map/ppermute | solution.py:23
  145.0 3.5 copy-start
  148.4 424.1 %all-reduce.19.cloned.1.call-start = ((), (), s32[]{:S(2)}) async-start(), calls=%async_computation.4 | async-start | bytes 1179648 | tf_op jit(solution)/shard_map/psum | solution.py:112
  153.0 135.1 %copy-start.8 = (f32[2,128]{1,0:T(2,128)S(1)}, f32[2,128]{1,0:T(2,128)}, u32[]{:S(2)}) copy-start(f32[2,128]{1,0:T(2,128)} %param.14) | copy-start | bytes 3076
  285.3 312.1 %copy-start.2 = (f32[128,512]{1,0:T(8,128)S(1)}, f32[128,512]{1,0:T(8,128)}, u32[]{:S(2)}) copy-start(f32[128,512]{1,0:T(8,128)} %all-reduce.13.cloned.1.call-done) | copy-start | bytes 786436
  287.8 453.8 %all-reduce.15.cloned.1.call-start = ((), (), s32[]{:S(2)}) async-start(), calls=%async_computation.2 | async-start | bytes 524288 | tf_op jit(solution)/shard_map/psum | solution.py:106
  572.5 25.7 %copy-start.3 = (f32[1024,128]{0,1:T(8,128)S(1)}, f32[1024,128]{0,1:T(8,128)}, u32[]{:S(2)}) copy-start(f32[1024,128]{0,1:T(8,128)} %get-tuple-element.10) | copy-start | bytes 1572868
  603.2 425.5 %all-reduce.17.cloned.1.call-start = ((), (), s32[]{:S(2)}) async-start(), calls=%async_computation.3 | async-start | bytes 1179648 | tf_op jit(solution)/shard_map/psum | solution.py:112
  741.6 312.1 %copy-start.1 = (f32[128,512]{1,0:T(8,128)S(1)}, f32[128,512]{1,0:T(8,128)}, u32[]{:S(2)}) copy-start(f32[128,512]{1,0:T(8,128)} %all-reduce.15.cloned.1.call-done) | copy-start | bytes 786436
  1028.8 25.8 %copy-start.4 = (f32[1024,128]{0,1:T(8,128)S(1)}, f32[1024,128]{0,1:T(8,128)}, u32[]{:S(2)}) copy-start(f32[1024,128]{0,1:T(8,128)} %get-tuple-element.6) | copy-start | bytes 1572868
Sparse Core Ops, SparseCore 0:
  148.6 136.6 all-reduce.12
  288.5 283.9 all-reduce.18
  603.4 138.2 all-reduce.14
  744.8 283.9 all-reduce.16
where the time goes:
time: 1060 us
  waiting for transfers between devices  875 us (83%)
  other arithmetic  64.7 us (6%)
  blocking collectives  54.5 us (5%)
  local copies, waits for them, and re-layouts  24.5 us (2%)
  starting transfers between devices  23.4 us (2%)
  between operations  13.6 us (1%)
    psum x2, waiting for transfers between devices, local(): observed_cols, inner_block = lax.psum((cols_part, inner_part), 'row')  569 us
    psum x2, waiting for transfers between devices, local(): observed_rows = lax.psum(rows_part, 'grp')  264 us
    all_to_all x1, blocking collectives, local(): lax.all_to_all(advanced, 'row', split_axis=1, concat_axis=0, tiled=True)  54.5 us
    ppermute x2, waiting for transfers between devices, extended_2(): lax.ppermute(lax.slice_in_dim(block, block.shape[dim] - width, None, axis...  39.3 us
    another operation x7, other arithmetic, local(): factor = jnp.linalg.cholesky(system)  24.8 us
  transfers between devices with their start and end apart: 8, of which 8 were waited for; matrix products, arithmetic and copies ran while one was open for 1% of the time, Pallas kernels for 0%

commit v1 on v0

v1 whole, which is shorter than its diff:
```python
import functools

import jax
import jax.numpy as jnp
from jax import lax
from jax.experimental import pallas as pl
from jax.experimental.pallas import tpu as pltpu
from jax.sharding import PartitionSpec as P

NX = 128
NY = 128
NCELL = NX * NY
OBS = 256
GROUPS = 16
MEMBERS = 32
ROWS = 32
HIGHEST = lax.Precision.HIGHEST
MESH = pl.DeviceIdType.MESH
VMEM = pl.BlockSpec(memory_space=pltpu.VMEM)
SMEM = pl.BlockSpec(memory_space=pltpu.SMEM)
VMEM_LIMIT = 48 * 1024 * 1024


def stencil_coefficients(u, v):
    x = lax.broadcasted_iota(jnp.int32, (NY, NX), 1)
    y = lax.broadcasted_iota(jnp.int32, (NY, NX), 0)
    u12 = u / 12.0
    v12 = v / 12.0
    return jnp.stack(
        [
            jnp.where(x < NX - 1, 0.1 - 8.0 * u12, 0.0),
            jnp.where(x > 0, 0.1 + 8.0 * u12, 0.0),
            jnp.where(x < NX - 2, u12, 0.0),
            jnp.where(x > 1, -u12, 0.0),
            jnp.where(y < NY - 1, 0.1 - 8.0 * v12, 0.0),
            jnp.where(y > 0, 0.1 + 8.0 * v12, 0.0),
            jnp.where(y < NY - 2, v12, 0.0),
            jnp.where(y > 1, -v12, 0.0),
        ],
        axis=1,
    )


def lane_slope(cf, q, yp1, ym1, yp2, ym2):
    return (
        cf[0:1] * pltpu.roll(q, NX - 1, 1)
        + cf[1:2] * pltpu.roll(q, 1, 1)
        + cf[2:3] * pltpu.roll(q, NX - 2, 1)
        + cf[3:4] * pltpu.roll(q, 2, 1)
        + cf[4:5] * yp1
        + cf[5:6] * ym1
        + cf[6:7] * yp2
        + cf[7:8] * ym2
        - 0.4 * q
    )


def lanes(y):
    return pl.ds(pl.multiple_of(y * NX, NX), NX)


def rows_kernel(obs_ref, c_ref, coef_ref, a_ref, aot_ref, q1_ref):
    def read(ref, y):
        return ref[:, lanes(jnp.clip(y, 0, NY - 1))]

    def slope(ref, y):
        return lane_slope(
            coef_ref[y],
            read(ref, y),
            read(ref, y + 1),
            read(ref, y - 1),
            read(ref, y + 2),
            read(ref, y - 2),
        )

    def first(y, carry):
        q1_ref[:, lanes(y)] = c_ref[:, lanes(y)] + slope(c_ref, y)
        return carry

    def second(y, carry):
        a_ref[:, lanes(y)] = 0.5 * (c_ref[:, lanes(y)] + q1_ref[:, lanes(y)] + slope(q1_ref, y))
        return carry

    lax.fori_loop(0, NY, first, 0, unroll=4)
    lax.fori_loop(0, NY, second, 0, unroll=4)

    lane = lax.broadcasted_iota(jnp.int32, (ROWS, NX), 1)
    quarter = lax.axis_index("row") % 4
    place = lax.broadcasted_iota(jnp.int32, (NX, NX), 0) // ROWS == quarter
    for update in range(2):

        def pick(j, acc):
            cell = obs_ref[update, j]
            block = a_ref[:, lanes(cell // NX)]
            turned = pltpu.roll(block, (j - cell % NX + NX) % NX, 1)
            return jnp.where(lane == j, turned, acc)

        acc = lax.fori_loop(0, NX, pick, jnp.zeros((ROWS, NX), jnp.float32), unroll=8)
        full = jnp.where(place, jnp.concatenate([acc] * 4, axis=0), 0.0)
        aot_ref[update * NX : (update + 1) * NX, :] = full.T


def advance_rows(obs_cells, cov, coefs):
    return pl.pallas_call(
        rows_kernel,
        out_shape=(
            jax.ShapeDtypeStruct((ROWS, NCELL), jnp.float32),
            jax.ShapeDtypeStruct((OBS, NX), jnp.float32),
        ),
        in_specs=[SMEM, VMEM, VMEM],
        out_specs=(VMEM, VMEM),
        scratch_shapes=[pltpu.VMEM((ROWS, NCELL), jnp.float32)],
        compiler_params=pltpu.CompilerParams(vmem_limit_bytes=VMEM_LIMIT),
    )(obs_cells, cov, coefs)


def drain(ref, sem):
    pltpu.make_async_copy(ref, ref, sem).wait()


def remote(src, dst, send_sem, recv_sem, grp, row):
    return pltpu.make_async_remote_copy(
        src_ref=src,
        dst_ref=dst,
        send_sem=send_sem,
        recv_sem=recv_sem,
        device_id={"grp": grp, "row": row},
        device_id_type=MESH,
    )


def chain_kernel(
    obs_ref, aot_ref, coef_ref, s_ref, yg_ref, yr_ref,
    pieces, ext, mid, yt, spart, sparts, srow, send_sem, recv_sem,
):
    g = lax.axis_index("grp")
    r = lax.axis_index("row")
    y_in, quarter = r // 4, r % 4
    low = y_in < 4

    def share(i, carry):
        to = lax.rem(r + i, MEMBERS)
        remote(
            aot_ref.at[pl.ds(pl.multiple_of(to * 8, 8), 8)],
            pieces.at[16 + r], send_sem.at[0], recv_sem.at[0], g, to,
        ).start()
        return carry

    lax.fori_loop(1, MEMBERS, share, 0)
    own = pltpu.make_async_copy(
        aot_ref.at[pl.ds(pl.multiple_of(r * 8, 8), 8)], pieces.at[16 + r], recv_sem.at[0]
    )
    own.start()
    side = jnp.where(low, g - 1, g + 1)
    slot = jnp.where(low, 12 + y_in, y_in - 4) * 4 + quarter
    has_side = (side >= 0) & (side < GROUPS)

    @pl.when(has_side)
    def _():
        def share_side(i, carry):
            to = lax.rem(r + i, MEMBERS)
            remote(
                aot_ref.at[pl.ds(pl.multiple_of(to * 8, 8), 8)],
                pieces.at[slot], send_sem.at[1], recv_sem.at[jnp.where(low, 2, 1)], side, to,
            ).start()
            return carry

        lax.fori_loop(0, MEMBERS, share_side, 0)

    @pl.when(g == 0)
    def _():
        pieces[0:16] = jnp.zeros((16, 8, NX), jnp.float32)

    @pl.when(g == GROUPS - 1)
    def _():
        pieces[48:64] = jnp.zeros((16, 8, NX), jnp.float32)

    drain(pieces.at[16:48], recv_sem.at[0])

    @pl.when(g > 0)
    def _():
        drain(pieces.at[0:16], recv_sem.at[1])

    @pl.when(g < GROUPS - 1)
    def _():
        drain(pieces.at[48:64], recv_sem.at[2])

    for y in range(16):
        ext[:, y * NX : (y + 1) * NX] = (
            pieces[4 * y] + pieces[4 * y + 1] + pieces[4 * y + 2] + pieces[4 * y + 3]
        )

    def at(ref, y):
        return ref[:, y * NX : (y + 1) * NX]

    def slope(ref, y):
        return lane_slope(
            coef_ref[y], at(ref, y), at(ref, y + 1), at(ref, y - 1), at(ref, y + 2), at(ref, y - 2)
        )

    for y in range(2, 14):
        mid[:, y * NX : (y + 1) * NX] = at(ext, y) + slope(ext, y)
    for y in range(4, 12):
        yt[:, (y - 4) * NX : (y - 3) * NX] = 0.5 * (at(ext, y) + at(mid, y) + slope(mid, y))

    yg_ref[r] = yt[...]

    def to_group(i, carry):
        to = lax.rem(r + i, MEMBERS)
        remote(yt, yg_ref.at[r], send_sem.at[2], recv_sem.at[3], g, to).start()
        return carry

    def to_columns(i, carry):
        grp = lax.rem(g + i // 2, GROUPS)
        row = 2 * g + i % 2
        src = yt.at[:, pl.ds(pl.multiple_of((i % 2) * 512, 512), 512)]
        here = (grp == g) & (row == r)

        @pl.when(here)
        def _():
            pltpu.make_async_copy(src, yr_ref.at[r], recv_sem.at[4]).start()

        @pl.when(jnp.logical_not(here))
        def _():
            remote(src, yr_ref.at[r], send_sem.at[3], recv_sem.at[4], grp, row).start()

        return carry

    cell = lax.broadcasted_iota(jnp.int32, (1024, OBS), 0)
    chosen = jnp.where(cell == obs_ref[...] - 1024 * g, 1.0, 0.0)
    spart[...] = jnp.dot(yt[...], chosen, precision=HIGHEST, preferred_element_type=jnp.float32)
    sparts[g] = spart[...]

    def to_groups(i, carry):
        to = lax.rem(g + i, GROUPS)
        remote(spart, sparts.at[g], send_sem.at[4], recv_sem.at[5], to, r).start()
        return carry

    lax.fori_loop(1, GROUPS, to_groups, 0)
    lax.fori_loop(1, MEMBERS, to_group, 0)
    lax.fori_loop(0, MEMBERS, to_columns, 0)
    drain(sparts.at[0:15], recv_sem.at[5])
    srow[...] = jnp.sum(sparts[...], axis=0)
    s_ref[r] = srow[...]

    def block_row(i, carry):
        to = lax.rem(r + i, MEMBERS)
        remote(srow, s_ref.at[r], send_sem.at[5], recv_sem.at[6], g, to).start()
        return carry

    lax.fori_loop(1, MEMBERS, block_row, 0)
    drain(s_ref.at[0:31], recv_sem.at[6])
    drain(yg_ref.at[0:31], recv_sem.at[3])
    drain(yr_ref.at[0:32], recv_sem.at[4])

    drain(pieces.at[0:31], send_sem.at[0])

    @pl.when(has_side)
    def _():
        drain(pieces.at[0:32], send_sem.at[1])

    drain(yg_ref.at[0:31], send_sem.at[2])

    @pl.when(r // 2 == g)
    def _():
        drain(yr_ref.at[0:31], send_sem.at[3])

    @pl.when(r // 2 != g)
    def _():
        drain(yr_ref.at[0:32], send_sem.at[3])

    drain(sparts.at[0:15], send_sem.at[4])
    drain(s_ref.at[0:31], send_sem.at[5])


def observation_chain(obs_row, aot, coef_ext):
    return pl.pallas_call(
        chain_kernel,
        out_shape=(
            jax.ShapeDtypeStruct((MEMBERS, 8, OBS), jnp.float32),
            jax.ShapeDtypeStruct((MEMBERS, 8, 1024), jnp.float32),
            jax.ShapeDtypeStruct((MEMBERS, 8, 512), jnp.float32),
        ),
        in_specs=[VMEM] * 3,
        out_specs=(VMEM,) * 3,
        scratch_shapes=[
            pltpu.VMEM((64, 8, NX), jnp.float32),
            pltpu.VMEM((8, 2048), jnp.float32),
            pltpu.VMEM((8, 2048), jnp.float32),
            pltpu.VMEM((8, 1024), jnp.float32),
            pltpu.VMEM((8, OBS), jnp.float32),
            pltpu.VMEM((GROUPS, 8, OBS), jnp.float32),
            pltpu.VMEM((8, OBS), jnp.float32),
            pltpu.SemaphoreType.DMA((6,)),
            pltpu.SemaphoreType.DMA((7,)),
        ],
        compiler_params=pltpu.CompilerParams(
            has_side_effects=True, vmem_limit_bytes=VMEM_LIMIT
        ),
    )(obs_row, aot, coef_ext)


def negative_inverse(ref):
    row_at = lax.broadcasted_iota(jnp.int32, (128, 128), 0)
    col_at = lax.broadcasted_iota(jnp.int32, (128, 128), 1)

    def step(k, carry):
        a = ref[...]
        row = ref[pl.ds(k, 1), :]
        in_col = col_at == k
        col = jnp.sum(jnp.where(in_col, a, 0.0), axis=1, keepdims=True)
        pivot = jnp.sum(jnp.where(in_col[0:1], row, 0.0), axis=1, keepdims=True)
        inv = 1.0 / pivot
        scaled = row * inv
        new = a - col * scaled
        new = jnp.where(in_col, col * inv, new)
        ref[...] = jnp.where(row_at == k, jnp.where(in_col[0:1], -inv, scaled), new)
        return carry

    lax.fori_loop(0, 128, step, 0)


def dot(a, b):
    return jnp.dot(a, b, precision=HIGHEST, preferred_element_type=jnp.float32)


def solve_kernel(s_ref, r_ref, var_ref, z_ref, first, second):
    diagonal = lax.broadcasted_iota(jnp.int32, (128, 128), 0) == lax.broadcasted_iota(
        jnp.int32, (128, 128), 1
    )
    s11 = s_ref[0:128, 0:128]
    s12 = s_ref[0:128, 128:256]
    s21 = s_ref[128:256, 0:128]
    s22 = s_ref[128:256, 128:256]
    first[...] = 0.5 * (s11 + s11.T) + jnp.where(diagonal, var_ref[0:1, :], 0.0)
    negative_inverse(first)
    inner = s22 + dot(s21, dot(first[...], s12))
    second[...] = 0.5 * (inner + inner.T) + jnp.where(diagonal, var_ref[1:2, :], 0.0)
    negative_inverse(second)
    r1 = r_ref[0:128, :]
    r2 = r_ref[128:256, :] + dot(s21, dot(first[...], r1))
    z2 = -dot(second[...], r2)
    z_ref[128:256, :] = z2
    z_ref[0:128, :] = -dot(first[...], r1 - dot(s12, z2))


def solve(s, r, var):
    return pl.pallas_call(
        solve_kernel,
        out_shape=jax.ShapeDtypeStruct((OBS, 512), jnp.float32),
        in_specs=[VMEM] * 3,
        out_specs=VMEM,
        scratch_shapes=[pltpu.VMEM((128, 128), jnp.float32)] * 2,
        compiler_params=pltpu.CompilerParams(vmem_limit_bytes=VMEM_LIMIT),
    )(s, r, var)


def column_slope(q, yp1, ym1, yp2, ym2, u12, v12):
    x = lax.broadcasted_iota(jnp.int32, (NX, NX), 0)
    xp1 = jnp.where(x < NX - 1, pltpu.roll(q, NX - 1, 0), 0.0)
    xm1 = jnp.where(x > 0, pltpu.roll(q, 1, 0), 0.0)
    xp2 = jnp.where(x < NX - 2, pltpu.roll(q, NX - 2, 0), 0.0)
    xm2 = jnp.where(x > 1, pltpu.roll(q, 2, 0), 0.0)
    along_x = 8.0 * (xp1 - xm1) - (xp2 - xm2)
    along_y = 8.0 * (yp1 - ym1) - (yp2 - ym2)
    laplace = xp1 + xm1 + yp1 + ym1 - 4.0 * q
    return 0.1 * laplace - u12 * along_x - v12 * along_y


def main_kernel(
    a_ref, u_ref, v_ref, yg_ref, z_ref, out_ref,
    ext, mid, fore, theirs, ub, vb, qh, ql, zh, zl_, send_sem, recv_sem,
):
    g = lax.axis_index("grp")
    r = lax.axis_index("row")
    y, lo = g // 2, g % 2
    me = lo * MEMBERS + r

    for c in range(2):

        def scatter(i, carry):
            to = lax.rem(me + i, 2 * MEMBERS)
            to_lo, to_r = to // MEMBERS, to % MEMBERS
            start = pl.multiple_of(to_r * 512 + to_lo * 256 + c * 128, 128)
            remote(
                a_ref.at[:, pl.ds(start, 128)], ext.at[c, 16 + me],
                send_sem.at[c], recv_sem.at[c], 2 * y + to_lo, to_r,
            ).start()
            return carry

        lax.fori_loop(1, 2 * MEMBERS, scatter, 0)
        pltpu.make_async_copy(
            a_ref.at[:, pl.ds(pl.multiple_of(r * 512 + lo * 256 + c * 128, 128), 128)],
            ext.at[c, 16 + me], recv_sem.at[c],
        ).start()

    for yy in range(20):
        ub[yy] = jnp.broadcast_to(u_ref[:, yy : yy + 1], (NX, NX))
        vb[yy] = jnp.broadcast_to(v_ref[:, yy : yy + 1], (NX, NX))
    for j in range(8):
        q = yg_ref[:, j * NX : (j + 1) * NX].T
        high = q.astype(jnp.bfloat16)
        qh[j] = high
        ql[j] = (q - high.astype(jnp.float32)).astype(jnp.bfloat16)
    z = z_ref[...]
    z_high = z.astype(jnp.bfloat16)
    zh[...] = z_high
    zl_[...] = (z - z_high.astype(jnp.float32)).astype(jnp.bfloat16)

    @pl.when(y == 0)
    def _():
        for c in range(2):
            ext[c, 0:16] = jnp.zeros((16, ROWS, NX), jnp.float32)

    @pl.when(y == 7)
    def _():
        for c in range(2):
            ext[c, 80:96] = jnp.zeros((16, ROWS, NX), jnp.float32)

    def up(c):
        return remote(
            ext.at[c, 64:80], ext.at[c, 0:16], send_sem.at[2 + c], recv_sem.at[2 + c], g + 2, r
        )

    def down(c):
        return remote(
            ext.at[c, 16:32], ext.at[c, 80:96], send_sem.at[4 + c], recv_sem.at[4 + c], g - 2, r
        )

    def trade(c):
        return remote(
            fore.at[c, 1 - lo], theirs.at[c], send_sem.at[6 + c], recv_sem.at[6 + c],
            2 * y + 1 - lo, r,
        )

    def grid_row(c, yy):
        return jnp.concatenate([ext[c, 4 * yy + k] for k in range(4)], axis=0)

    def correct(column, j, field):
        at = pl.ds(column, 128)
        a_high, a_low, b_high, b_low = qh[j], ql[j], zh[:, at], zl_[:, at]

        def part(a, b):
            return jnp.dot(a, b, preferred_element_type=jnp.float32)

        out_ref[pl.ds(pl.multiple_of(j * NX, NX), NX), at] = field - (
            part(a_high, b_high) + part(a_high, b_low) + part(a_low, b_high)
        )

    for c in range(2):
        drain(ext.at[c, 16:80], recv_sem.at[c])

        @pl.when(y < 7)
        def _():
            up(c).start()

        @pl.when(y > 0)
        def _():
            down(c).start()

    for c in range(2):

        @pl.when(y > 0)
        def _():
            up(c).wait_recv()

        @pl.when(y < 7)
        def _():
            down(c).wait_recv()

        def first(yy, carry):
            q = grid_row(c, yy)
            inside = (y * 16 + yy - 4 >= 0) & (y * 16 + yy - 4 < NY)
            step = column_slope(
                q, grid_row(c, yy + 1), grid_row(c, yy - 1), grid_row(c, yy + 2),
                grid_row(c, yy - 2), ub[yy - 2], vb[yy - 2],
            )
            mid[yy - 2] = jnp.where(inside, q + step, 0.0)
            return carry

        def second(yy, carry):
            q1 = mid[yy - 2]
            step = column_slope(
                q1, mid[yy - 1], mid[yy - 3], mid[yy], mid[yy - 4], ub[yy - 2], vb[yy - 2]
            )
            at = yy - 4
            fore[c, at // 8, at % 8] = 0.5 * (grid_row(c, yy) + q1 + step)
            return carry

        lax.fori_loop(2, 22, first, 0)
        lax.fori_loop(4, 20, second, 0)
        trade(c).start()
        mine = pl.multiple_of(lo * 256 + c * 128, 128)

        def finish(j, carry):
            correct(mine, j, fore[c, lo, j])
            return carry

        lax.fori_loop(0, 8, finish, 0)

    for c in range(2):
        trade(c).wait_recv()
        other = pl.multiple_of((1 - lo) * 256 + c * 128, 128)

        def finish_other(j, carry):
            correct(other, j, theirs[c, j])
            return carry

        lax.fori_loop(0, 8, finish_other, 0)

    for c in range(2):
        drain(ext.at[c, 0:63], send_sem.at[c])
        trade(c).wait_send()

        @pl.when(y < 7)
        def _():
            up(c).wait_send()

        @pl.when(y > 0)
        def _():
            down(c).wait_send()


def exchange_and_correct(a, u_ext, v_ext, yg, z):
    f32, bf16 = jnp.float32, jnp.bfloat16
    return pl.pallas_call(
        main_kernel,
        out_shape=jax.ShapeDtypeStruct((1024, 512), f32),
        in_specs=[VMEM] * 5,
        out_specs=VMEM,
        scratch_shapes=[
            pltpu.VMEM((2, 96, ROWS, NX), f32),
            pltpu.VMEM((20, NX, NX), f32),
            pltpu.VMEM((2, 2, 8, NX, NX), f32),
            pltpu.VMEM((2, 8, NX, NX), f32),
            pltpu.VMEM((20, NX, NX), f32),
            pltpu.VMEM((20, NX, NX), f32),
            pltpu.VMEM((8, NX, OBS), bf16),
            pltpu.VMEM((8, NX, OBS), bf16),
            pltpu.VMEM((OBS, 512), bf16),
            pltpu.VMEM((OBS, 512), bf16),
            pltpu.SemaphoreType.DMA((8,)),
            pltpu.SemaphoreType.DMA((8,)),
        ],
        compiler_params=pltpu.CompilerParams(
            has_side_effects=True, vmem_limit_bytes=VMEM_LIMIT
        ),
    )(a, u_ext, v_ext, yg, z)


def local(cov_prior, courant_x_field, courant_y_field, obs_cells, obs_var):
    g = lax.axis_index("grp")
    coefs = stencil_coefficients(courant_x_field, courant_y_field)
    advanced, aot = advance_rows(obs_cells, cov_prior, coefs)
    coef_ext = lax.dynamic_slice_in_dim(
        jnp.pad(coefs, ((4, 4), (0, 0), (0, 0))), g * 8, 16, 0
    )
    s, yg, yr = observation_chain(obs_cells.reshape(1, OBS), aot, coef_ext)
    z = solve(s.reshape(OBS, OBS), yr.reshape(OBS, 512), obs_var)

    def columns(field):
        padded = jnp.pad(field / 12.0, ((2, 2), (0, 0)))
        return lax.dynamic_slice_in_dim(padded, (g // 2) * 16, 20, 0).T

    return exchange_and_correct(
        advanced, columns(courant_x_field), columns(courant_y_field), yg.reshape(OBS, 1024), z
    )


def solution(mesh):
    placed = (P(("grp", "row"), None), P(), P(), P(), P())
    return jax.shard_map(
        local, mesh=mesh, in_specs=placed, out_specs=P("grp", "row"), check_vma=False
    )
```

time: 1060 us -> 222 us (0.21)
  the two profiles are of different devices: /device:TPU:8 before, /device:TPU:70 now
where the time goes in v1:
time: 222 us
  Pallas kernels  217 us (98%)
  local copies, waits for them, and re-layouts  4.27 us (2%)
    pallas_call x1, Pallas kernels, exchange_and_correct(): pl.pallas_call(main_kernel, out_shape=jax.ShapeDtypeStruct((1024, 512), f...  99.3 us
    pallas_call x1, Pallas kernels, observation_chain(): pl.pallas_call(chain_kernel, out_shape=(jax.ShapeDtypeStruct((MEMBERS, 8,...  74.2 us
    pallas_call x1, Pallas kernels, solve(): pl.pallas_call(solve_kernel, out_shape=jax.ShapeDtypeStruct((OBS, 512), j...  28.9 us
    pallas_call x1, Pallas kernels, advance_rows(): pl.pallas_call(rows_kernel, out_shape=(jax.ShapeDtypeStruct((ROWS, NCELL)...  14.9 us

profile of v1, /device:TPU:70, one launch (start us, length us, event | category | flops | bytes accessed | tf_op | source)
XLA Modules:
  0.0 222.1 jit_solution(16322085652260661686)
XLA Ops:
  0.0 0.9 copy.6
  1.0 0.9 copy.8
  1.9 0.0 copy-start
  1.9 0.0 copy-start.1
  2.0 0.1 fusion
  2.1 0.1 bitcast_dynamic-update-slice_fusion.7
  2.2 0.1 bitcast_dynamic-update-slice_fusion.6
  2.3 0.1 bitcast_dynamic-update-slice_fusion.5
  2.4 0.1 bitcast_dynamic-update-slice_fusion.4
  2.5 0.2 pad_dynamic-slice_fusion
  2.7 0.0 copy-start.2
  2.8 0.2 copy.11.coef_ref
  2.9 0.2 copy.10.coef_ref
  3.2 0.4 copy-done
  3.5 0.0 copy-done.1
  3.5 14.9 %shard_map.55 = (f32[32,16384]{1,0:T(8,128)S(1)}, f32[256,128]{1,0:T(8,128)S(1)}) custom-call(s32[2,128]{1,0:T(2,128)S(1)} %copy-done.1, f32[32,16384]{1,0:T(8,128)S(1)} %copy-done, f32[128,8,128]{2,1,0:T(8,128)S(1)} %copy.10.coef_ref), custom_call_target="tpu_custom_call" | custom-call | tf_op jit(solution)/shard_map/pallas_call | solution.py:104
  18.4 74.2 %shard_map.56 = (f32[32,8,256]{2,1,0:T(8,128)S(1)}, f32[32,8,1024]{2,1,0:T(8,128)S(1)}, f32[32,8,512]{2,1,0:T(8,128)S(1)}) custom-call(s32[1,256]{1,0:T(1,128)S(1)} %bitcast.27, f32[256,128]{1,0:T(8,128)S(1)} %get-tuple-element.11.aot_ref, f32[16,8,128]{2,1,0:T(8,128)S(1)} %copy.11.coef_ref), custom_call_target="tpu_custom_call" | custom-call | tf_op jit(solution)/shard_map/pallas_call | solution.py:277
  92.6 0.0 copy-done.2
  92.6 28.9 %shard_map.57.z_ref = f32[256,512]{1,0:T(8,128)S(1)} custom-call(f32[256,256]{1,0:T(8,128)S(1)} %bitcast.26, f32[256,512]{1,0:T(8,128)S(1)} %bitcast.25, f32[2,128]{1,0:T(2,128)S(1)} %copy-done.2), custom_call_target="tpu_custom_call" | custom-call | tf_op jit(solution)/shard_map/pallas_call | solution.py:348
  121.5 99.3 %shard_map.58 = f32[1024,512]{1,0:T(8,128)S(1)} custom-call(f32[32,16384]{1,0:T(8,128)S(1)} %get-tuple-element.10.a_ref, f32[128,20]{1,0:T(8,128)S(1)} %get-tuple-element.15.u_ref, f32[128,20]{1,0:T(8,128)S(1)} %get-tuple-element.16.v_ref, f32[256,1024]{1,0:T(8,128)S(1)} %bitcast.24, f32[256,512]{1,0:T(8,128)S(1)} %shard_map.57.z_ref), custom_call_target="tpu_custom_call" | custom-call | tf_op jit(solution)/shard_map/pallas_call | solution.py:526
  220.8 1.3 copy.20
  (10 shorter events, 0.1 us)
Async XLA Ops:
  1.9 1.6 copy-start
  1.9 1.6 copy-start.1
  2.7 89.8 %copy-start.2 = (f32[2,128]{1,0:T(2,128)S(1)}, f32[2,128]{1,0:T(2,128)}, u32[]{:S(2)}) copy-start(f32[2,128]{1,0:T(2,128)} %var_ref.1) | copy-start | bytes 3076

commit v2 on v0

v2 whole, which is shorter than its diff:
```python
import jax
import jax.numpy as jnp
from jax import lax
from jax.experimental import pallas as pl
from jax.experimental.pallas import tpu as pltpu
from jax.sharding import PartitionSpec as P

NX = 128
NY = 128
NCELL = NX * NY
OBS = 256
GROUPS = 16
MEMBERS = 32
ROWS = 32
HIGHEST = lax.Precision.HIGHEST
MESH = pl.DeviceIdType.MESH
VMEM = pl.BlockSpec(memory_space=pltpu.VMEM)
VMEM_LIMIT = 48 * 1024 * 1024


def lane_slope(cf, q, yp1, ym1, yp2, ym2):
    return (
        cf[0] * pltpu.roll(q, NX - 1, 1)
        + cf[1] * pltpu.roll(q, 1, 1)
        + cf[2] * pltpu.roll(q, NX - 2, 1)
        + cf[3] * pltpu.roll(q, 2, 1)
        + cf[4] * yp1
        + cf[5] * ym1
        + cf[6] * yp2
        + cf[7] * ym2
        - 0.4 * q
    )


def lanes(y):
    return pl.ds(pl.multiple_of(y * NX, NX), NX)


def drain(ref, sem):
    pltpu.make_async_copy(ref, ref, sem).wait()


def remote(src, dst, send_sem, recv_sem, grp, row):
    return pltpu.make_async_remote_copy(
        src_ref=src,
        dst_ref=dst,
        send_sem=send_sem,
        recv_sem=recv_sem,
        device_id={"grp": grp, "row": row},
        device_id_type=MESH,
    )


def negative_inverse(ref):
    row_at = lax.broadcasted_iota(jnp.int32, (128, 128), 0)
    col_at = lax.broadcasted_iota(jnp.int32, (128, 128), 1)

    def step(k, carry):
        a = ref[...]
        row = ref[pl.ds(k, 1), :]
        in_col = col_at == k
        col = jnp.sum(jnp.where(in_col, a, 0.0), axis=1, keepdims=True)
        pivot = jnp.sum(jnp.where(in_col[0:1], row, 0.0), axis=1, keepdims=True)
        inv = 1.0 / pivot
        scaled = row * inv
        new = a - col * scaled
        new = jnp.where(in_col, col * inv, new)
        ref[...] = jnp.where(row_at == k, jnp.where(in_col[0:1], -inv, scaled), new)
        return carry

    lax.fori_loop(0, 128, step, 0)


def dot(a, b):
    return jnp.dot(a, b, precision=HIGHEST, preferred_element_type=jnp.float32)


def dot(a, b):
    return jnp.dot(a, b, precision=HIGHEST, preferred_element_type=jnp.float32)


def column_slope(q, yp1, ym1, yp2, ym2, u12, v12):
    x = lax.broadcasted_iota(jnp.int32, (NX, NX), 0)
    xp1 = jnp.where(x < NX - 1, pltpu.roll(q, NX - 1, 0), 0.0)
    xm1 = jnp.where(x > 0, pltpu.roll(q, 1, 0), 0.0)
    xp2 = jnp.where(x < NX - 2, pltpu.roll(q, NX - 2, 0), 0.0)
    xm2 = jnp.where(x > 1, pltpu.roll(q, 2, 0), 0.0)
    along_x = 8.0 * (xp1 - xm1) - (xp2 - xm2)
    along_y = 8.0 * (yp1 - ym1) - (yp2 - ym2)
    laplace = xp1 + xm1 + yp1 + ym1 - 4.0 * q
    return 0.1 * laplace - u12 * along_x - v12 * along_y


def kernel(
    obs_row_ref, c_ref, u_ref, v_ref, var_ref, out_ref,
    coef, q1, adv, aot, pieces, near, mid8, yt, rt, spart, sparts, srow, s_all, yg, yr, first, second,
    ext, mid, fore, theirs, ub, vb, qh, ql, zh, zl, send_sem, recv_sem,
):
    f32, bf16 = jnp.float32, jnp.bfloat16
    g = lax.axis_index("grp")
    r = lax.axis_index("row")
    y, lo = g // 2, g % 2
    chip, core = r // 2, r % 2
    me = lo * MEMBERS + r

    barrier = pltpu.get_barrier_semaphore()

    def greet(grp, row):
        pl.semaphore_signal(
            barrier, inc=1, device_id={"grp": grp, "row": row}, device_id_type=MESH
        )

    def greet_plane(i, carry):
        to = lax.rem(me + i, 2 * MEMBERS)
        greet(2 * y + to // MEMBERS, to % MEMBERS)
        return carry

    lax.fori_loop(1, 2 * MEMBERS, greet_plane, 0)
    across = jnp.where(lo == 0, g - 1, g + 1)
    has_across = (across >= 0) & (across < GROUPS)

    @pl.when(has_across)
    def _():
        def greet_across(i, carry):
            greet(across, i)
            return carry

        lax.fori_loop(0, MEMBERS, greet_across, 0)

    def greet_planes(i, carry):
        greet(lax.rem(2 * y + 2 + i // 2, GROUPS), 2 * chip + i % 2)
        return carry

    lax.fori_loop(0, 2 * GROUPS - 4, greet_planes, 0)
    on_diagonal = chip == g

    @pl.when(jnp.logical_not(on_diagonal))
    def _():
        greet(chip, 2 * g + core)

    gx = lax.broadcasted_iota(jnp.int32, (NY, NX), 1)
    gy = lax.broadcasted_iota(jnp.int32, (NY, NX), 0)
    u12 = u_ref[...] * (1.0 / 12.0)
    v12 = v_ref[...] * (1.0 / 12.0)
    factors = (
        jnp.where(gx < NX - 1, 0.1 - 8.0 * u12, 0.0),
        jnp.where(gx > 0, 0.1 + 8.0 * u12, 0.0),
        jnp.where(gx < NX - 2, u12, 0.0),
        jnp.where(gx > 1, -u12, 0.0),
        jnp.where(gy < NY - 1, 0.1 - 8.0 * v12, 0.0),
        jnp.where(gy > 0, 0.1 + 8.0 * v12, 0.0),
        jnp.where(gy < NY - 2, v12, 0.0),
        jnp.where(gy > 1, -v12, 0.0),
    )
    for k in range(8):
        coef[k, 0:8] = jnp.zeros((8, NX), f32)
        coef[k, 128:136] = jnp.zeros((8, NX), f32)
        coef[k, 4 : 4 + NY] = factors[k]

    def factors_at(row):
        return [coef[k, pl.ds(row, 1), :] for k in range(8)]

    def read(ref, yy):
        return ref[:, lanes(jnp.clip(yy, 0, NY - 1))]

    def row_slope(ref, yy):
        return lane_slope(
            factors_at(yy + 4), read(ref, yy), read(ref, yy + 1), read(ref, yy - 1),
            read(ref, yy + 2), read(ref, yy - 2),
        )

    def row_first(yy, carry):
        q1[:, lanes(yy)] = c_ref[:, lanes(yy)] + row_slope(c_ref, yy)
        return carry

    cells = obs_row_ref[...]
    chosen_x = jnp.where(
        lax.broadcasted_iota(jnp.int32, (NX, OBS), 0) == cells % NX, 1.0, 0.0
    ).astype(bf16)
    cells_y = cells // NX

    def row_second(yy, acc):
        new = 0.5 * (c_ref[:, lanes(yy)] + q1[:, lanes(yy)] + row_slope(q1, yy))
        adv[:, lanes(yy)] = new
        high = new.astype(bf16)
        rest = new - high.astype(f32)
        middle = rest.astype(bf16)
        low = (rest - middle.astype(f32)).astype(bf16)
        parts = jnp.dot(
            jnp.concatenate([high, middle, low], axis=0), chosen_x, preferred_element_type=f32
        )
        found = parts[0:ROWS] + (parts[ROWS : 2 * ROWS] + parts[2 * ROWS :])
        return jnp.where(cells_y == yy, found, acc)

    lax.fori_loop(0, NY, row_first, 0, unroll=4)
    acc = lax.fori_loop(0, NY, row_second, jnp.zeros((ROWS, OBS), f32), unroll=4)

    quarter = r % 4
    place = lax.broadcasted_iota(jnp.int32, (NX, NX), 0) // ROWS == quarter
    for update in range(2):
        part = acc[:, update * NX : (update + 1) * NX]
        full = jnp.where(place, jnp.concatenate([part] * 4, axis=0), 0.0)
        aot[update * NX : (update + 1) * NX, :] = full.T

    pl.semaphore_wait(
        barrier,
        2 * MEMBERS - 1 + 2 * GROUPS - 4
        + jnp.where(has_across, MEMBERS, 0) + jnp.where(on_diagonal, 0, 1),
    )

    def some(to):
        return aot.at[pl.ds(pl.multiple_of(to * 8, 8), 8)]

    def share(i, carry):
        to = lax.rem(r + i, MEMBERS)
        remote(some(to), pieces.at[16 + r], send_sem.at[0], recv_sem.at[0], g, to).start()
        return carry

    lax.fori_loop(1, MEMBERS, share, 0)
    pltpu.make_async_copy(some(r), pieces.at[16 + r], recv_sem.at[0]).start()
    y_in = r // 4
    low = y_in < 4
    side = jnp.where(low, g - 1, g + 1)
    slot = jnp.where(low, 12 + y_in, y_in - 4) * 4 + quarter
    has_side = (side >= 0) & (side < GROUPS)

    @pl.when(has_side)
    def _():
        def share_side(i, carry):
            to = lax.rem(r + i, MEMBERS)
            remote(
                some(to), pieces.at[slot], send_sem.at[1], recv_sem.at[jnp.where(low, 2, 1)], side, to
            ).start()
            return carry

        lax.fori_loop(0, MEMBERS, share_side, 0)

    def my_columns(c):
        return adv.at[:, pl.ds(pl.multiple_of(r * 512 + lo * 256 + c * 128, 128), 128)]

    def scatter(c):
        def send(i, carry):
            to = lax.rem(me + i, 2 * MEMBERS)
            to_lo, to_r = to // MEMBERS, to % MEMBERS
            start = pl.multiple_of(to_r * 512 + to_lo * 256 + c * 128, 128)
            remote(
                adv.at[:, pl.ds(start, 128)], ext.at[c, 16 + me],
                send_sem.at[6 + c], recv_sem.at[7 + c], 2 * y + to_lo, to_r,
            ).start()
            return carry

        lax.fori_loop(1, 2 * MEMBERS, send, 0)
        pltpu.make_async_copy(my_columns(c), ext.at[c, 16 + me], recv_sem.at[7 + c]).start()

    scatter(0)

    ut = pltpu.roll(u12.T, lax.rem(2 * NX - 16 * y + 2, NX), 1)
    vt = pltpu.roll(v12.T, lax.rem(2 * NX - 16 * y + 2, NX), 1)
    for k in range(20):
        ub[k] = jnp.broadcast_to(ut[:, k : k + 1], (NX, NX))
        vb[k] = jnp.broadcast_to(vt[:, k : k + 1], (NX, NX))

    @pl.when(g == 0)
    def _():
        pieces[0:16] = jnp.zeros((16, 8, NX), f32)

    @pl.when(g == GROUPS - 1)
    def _():
        pieces[48:64] = jnp.zeros((16, 8, NX), f32)

    @pl.when(y == 0)
    def _():
        for c in range(2):
            ext[c, 0:16] = jnp.zeros((16, ROWS, NX), f32)

    @pl.when(y == 7)
    def _():
        for c in range(2):
            ext[c, 80:96] = jnp.zeros((16, ROWS, NX), f32)

    drain(pieces.at[16:48], recv_sem.at[0])

    @pl.when(g > 0)
    def _():
        drain(pieces.at[0:16], recv_sem.at[1])

    @pl.when(g < GROUPS - 1)
    def _():
        drain(pieces.at[48:64], recv_sem.at[2])

    for k in range(16):
        near[:, k * NX : (k + 1) * NX] = (
            pieces[4 * k] + pieces[4 * k + 1] + pieces[4 * k + 2] + pieces[4 * k + 3]
        )

    def at(ref, k):
        return ref[:, k * NX : (k + 1) * NX]

    def near_slope(ref, k):
        return lane_slope(
            factors_at(8 * g + k), at(ref, k), at(ref, k + 1), at(ref, k - 1),
            at(ref, k + 2), at(ref, k - 2),
        )

    for k in range(2, 14):
        mid8[:, k * NX : (k + 1) * NX] = at(near, k) + near_slope(near, k)
    for k in range(4, 12):
        yt[:, (k - 4) * NX : (k - 3) * NX] = 0.5 * (at(near, k) + at(mid8, k) + near_slope(mid8, k))

    cell_at = lax.broadcasted_iota(jnp.int32, (1024, OBS), 0)
    chosen = jnp.where(cell_at == obs_row_ref[...] - 1024 * g, 1.0, 0.0)
    spart[...] = dot(yt[...], chosen)
    sparts[g] = spart[...]

    def to_groups(i, carry):
        to = lax.rem(g + i, GROUPS)
        remote(spart, sparts.at[g], send_sem.at[2], recv_sem.at[3], to, r).start()
        return carry

    lax.fori_loop(1, GROUPS, to_groups, 0)

    @pl.when(on_diagonal)
    def _():
        pltpu.make_async_copy(yt, rt, recv_sem.at[5]).start()

    @pl.when(jnp.logical_not(on_diagonal))
    def _():
        remote(yt, rt, send_sem.at[4], recv_sem.at[5], chip, 2 * g + core).start()

    yg[chip, core] = yt[...]

    def to_group(i, carry):
        to = lax.rem(r + 2 * i, MEMBERS)
        remote(yt, yg.at[chip, core], send_sem.at[5], recv_sem.at[6], g, to).start()
        return carry

    lax.fori_loop(1, GROUPS, to_group, 0)
    drain(sparts.at[0:15], recv_sem.at[3])
    srow[...] = jnp.sum(sparts[...], axis=0)
    s_all[r] = srow[...]

    def block_row(i, carry):
        to = lax.rem(r + i, MEMBERS)
        remote(srow, s_all.at[r], send_sem.at[3], recv_sem.at[4], g, to).start()
        return carry

    lax.fori_loop(1, MEMBERS, block_row, 0)

    drain(rt, recv_sem.at[5])

    def to_columns(i, carry):
        grp = lax.rem(g + i // 2, GROUPS)
        half = lax.rem(core + i, 2)
        remote(
            rt.at[:, pl.ds(pl.multiple_of(half * 512, 512), 512)], yr.at[2 * g + core],
            send_sem.at[8], recv_sem.at[9], grp, 2 * chip + half,
        ).start()
        return carry

    lax.fori_loop(1, 2 * GROUPS, to_columns, 0)
    pltpu.make_async_copy(
        rt.at[:, pl.ds(pl.multiple_of(core * 512, 512), 512)], yr.at[2 * g + core], recv_sem.at[9]
    ).start()
    scatter(1)

    drain(s_all.at[0:31], recv_sem.at[4])
    diagonal = lax.broadcasted_iota(jnp.int32, (128, 128), 0) == lax.broadcasted_iota(
        jnp.int32, (128, 128), 1
    )
    s11 = s_all[0:16, :, 0:128].reshape(128, 128)
    first[...] = 0.5 * (s11 + s11.T) + jnp.where(diagonal, var_ref[0:1, :], 0.0)
    negative_inverse(first)

    drain(yg.at[0:15, 0], recv_sem.at[6])
    relay = remote(
        yg.at[:, core], yg.at[:, core], send_sem.at[9], recv_sem.at[10], g, 2 * chip + 1 - core
    )
    relay.start()

    def up(c):
        return remote(
            ext.at[c, 64:80], ext.at[c, 0:16], send_sem.at[10 + c], recv_sem.at[11 + c], g + 2, r
        )

    def down(c):
        return remote(
            ext.at[c, 16:32], ext.at[c, 80:96], send_sem.at[12 + c], recv_sem.at[13 + c], g - 2, r
        )

    def trade(c):
        return remote(
            fore.at[c, 1 - lo], theirs.at[c], send_sem.at[14 + c], recv_sem.at[15 + c],
            2 * y + 1 - lo, r,
        )

    def start_halo(c):
        drain(ext.at[c, 16:80], recv_sem.at[7 + c])

        @pl.when(y < 7)
        def _():
            up(c).start()

        @pl.when(y > 0)
        def _():
            down(c).start()

    start_halo(0)

    s12 = s_all[0:16, :, 128:256].reshape(128, 128)
    s21 = s_all[16:32, :, 0:128].reshape(128, 128)
    s22 = s_all[16:32, :, 128:256].reshape(128, 128)
    inner = s22 + dot(s21, dot(first[...], s12))
    second[...] = 0.5 * (inner + inner.T) + jnp.where(diagonal, var_ref[1:2, :], 0.0)
    negative_inverse(second)
    drain(yr, recv_sem.at[9])
    r1 = yr[0:16].reshape(128, 512)
    r2 = yr[16:32].reshape(128, 512)
    z2 = -dot(second[...], r2 + dot(s21, dot(first[...], r1)))
    z1 = -dot(first[...], r1 - dot(s12, z2))
    for k, z in ((0, z1), (1, z2)):
        high = z.astype(bf16)
        zh[k * 128 : (k + 1) * 128, :] = high
        zl[k * 128 : (k + 1) * 128, :] = (z - high.astype(f32)).astype(bf16)
    relay.wait_recv()
    for j in range(8):
        q = yg[:, :, :, j * NX : (j + 1) * NX].reshape(OBS, NX).T
        high = q.astype(bf16)
        qh[j] = high
        ql[j] = (q - high.astype(f32)).astype(bf16)

    def grid_row(c, k):
        return jnp.concatenate([ext[c, 4 * k + i] for i in range(4)], axis=0)

    def column_first(c, start, stop):
        def step(k, carry):
            q = grid_row(c, k)
            inside = (y * 16 + k - 4 >= 0) & (y * 16 + k - 4 < NY)
            slope = column_slope(
                q, grid_row(c, k + 1), grid_row(c, k - 1), grid_row(c, k + 2), grid_row(c, k - 2),
                ub[k - 2], vb[k - 2],
            )
            mid[k - 2] = jnp.where(inside, q + slope, 0.0)
            return carry

        lax.fori_loop(start, stop, step, 0)

    def column_second(c, half):
        def step(j, carry):
            k = half * 8 + j + 4
            q = mid[k - 2]
            slope = column_slope(
                q, mid[k - 1], mid[k - 3], mid[k], mid[k - 4], ub[k - 2], vb[k - 2]
            )
            fore[c, half, j] = 0.5 * (grid_row(c, k) + q + slope)
            return carry

        lax.fori_loop(0, 8, step, 0)

    def correct(column, field):
        cols = pl.ds(pl.multiple_of(column, 128), 128)
        b_high, b_low = zh[:, cols], zl[:, cols]

        def part(a, b):
            return jnp.dot(a, b, preferred_element_type=f32)

        def step(j, carry):
            a_high, a_low = qh[j], ql[j]
            out_ref[pl.ds(pl.multiple_of(j * NX, NX), NX), cols] = field(j) - (
                part(a_high, b_high) + part(a_high, b_low) + part(a_low, b_high)
            )
            return carry

        lax.fori_loop(0, 8, step, 0)

    for c in range(2):
        if c == 1:
            start_halo(1)
        column_first(c, 6, 18)

        @pl.when(y > 0)
        def _():
            up(c).wait_recv()

        @pl.when(y < 7)
        def _():
            down(c).wait_recv()

        column_first(c, 2, 6)
        column_first(c, 18, 22)
        column_second(c, 1 - lo)
        trade(c).start()
        column_second(c, lo)
        correct(lo * 256 + c * 128, lambda j: fore[c, lo, j])
    for c in range(2):
        trade(c).wait_recv()
        correct((1 - lo) * 256 + c * 128, lambda j: theirs[c, j])

    drain(pieces.at[0:31], send_sem.at[0])

    @pl.when(has_side)
    def _():
        drain(pieces.at[0:32], send_sem.at[1])

    drain(sparts.at[0:15], send_sem.at[2])
    drain(s_all.at[0:31], send_sem.at[3])

    @pl.when(jnp.logical_not(on_diagonal))
    def _():
        drain(rt, send_sem.at[4])

    drain(yg.at[0:15, 0], send_sem.at[5])
    drain(yr.at[0:31], send_sem.at[8])
    relay.wait_send()
    for c in range(2):
        drain(ext.at[c, 0:63], send_sem.at[6 + c])
        trade(c).wait_send()

        @pl.when(y < 7)
        def _():
            up(c).wait_send()

        @pl.when(y > 0)
        def _():
            down(c).wait_send()


def local(cov_prior, courant_x_field, courant_y_field, obs_cells, obs_var):
    f32, bf16 = jnp.float32, jnp.bfloat16
    scratch = [
        ((8, 136, NX), f32),
        ((ROWS, NCELL), f32),
        ((ROWS, NCELL), f32),
        ((OBS, NX), f32),
        ((64, 8, NX), f32),
        ((8, 2048), f32),
        ((8, 2048), f32),
        ((8, 1024), f32),
        ((8, 1024), f32),
        ((8, OBS), f32),
        ((GROUPS, 8, OBS), f32),
        ((8, OBS), f32),
        ((MEMBERS, 8, OBS), f32),
        ((GROUPS, 2, 8, 1024), f32),
        ((MEMBERS, 8, 512), f32),
        ((128, 128), f32),
        ((128, 128), f32),
        ((2, 96, ROWS, NX), f32),
        ((20, NX, NX), f32),
        ((2, 2, 8, NX, NX), f32),
        ((2, 8, NX, NX), f32),
        ((20, NX, NX), f32),
        ((20, NX, NX), f32),
        ((8, NX, OBS), bf16),
        ((8, NX, OBS), bf16),
        ((OBS, 512), bf16),
        ((OBS, 512), bf16),
    ]
    return pl.pallas_call(
        kernel,
        out_shape=jax.ShapeDtypeStruct((1024, 512), f32),
        in_specs=[VMEM] * 5,
        out_specs=VMEM,
        scratch_shapes=[pltpu.VMEM(shape, dtype) for shape, dtype in scratch]
        + [pltpu.SemaphoreType.DMA((16,)), pltpu.SemaphoreType.DMA((17,))],
        compiler_params=pltpu.CompilerParams(
            collective_id=0, has_side_effects=True, vmem_limit_bytes=VMEM_LIMIT
        ),
    )(obs_cells.reshape(1, OBS), cov_prior, courant_x_field, courant_y_field, obs_var)


def solution(mesh):
    placed = (P(("grp", "row"), None), P(), P(), P(), P())
    return jax.shard_map(
        local, mesh=mesh, in_specs=placed, out_specs=P("grp", "row"), check_vma=False
    )
```

time: 1060 us -> 158 us (0.15)
  the two profiles are of different devices: /device:TPU:8 before, /device:TPU:30 now
where the time goes in v2:
time: 158 us
  Pallas kernels  152 us (96%)
  local copies, waits for them, and re-layouts  5.95 us (4%)
    pallas_call x1, Pallas kernels, local(): pl.pallas_call(kernel, out_shape=jax.ShapeDtypeStruct((1024, 512), f32),...  152 us
    unnamed x11, local copies, waits for them, and re-layouts  5.95 us

profile of v2, /device:TPU:30, one launch (start us, length us, event | category | flops | bytes accessed | tf_op | source)
XLA Modules:
  0.0 158.1 jit_solution(15453671821061554546)
XLA Ops:
  0.0 0.0 copy-start
  0.0 1.6 %copy-done = f32[32,16384]{1,0:T(8,128)S(1)} copy-done((f32[32,16384]{1,0:T(8,128)S(1)}, f32[32,16384]{1,0:T(8,128)}, u32[]{:S(2)}) %copy-start) | copy-done | bytes 2097176
  1.6 0.0 copy-start.1
  1.6 0.8 copy-done.1
  2.4 0.0 copy-start.2
  2.4 0.8 copy-done.2
  3.3 0.0 copy-start.3
  3.3 0.7 copy-done.3
  4.0 0.0 copy-start.4
  4.0 0.7 copy-done.4
  4.6 152.1 %shard_map.55 = f32[1024,512]{1,0:T(8,128)S(1)} custom-call(s32[1,256]{1,0:T(1,128)S(1)} %bitcast.1, f32[32,16384]{1,0:T(8,128)S(1)} %copy-done, f32[128,128]{1,0:T(8,128)S(1)} %copy-done.1, f32[128,128]{1,0:T(8,128)S(1)} %copy-done.2, f32[2,128]{1,0:T(2,128)S(1)} %copy-done.4), custom_call_target="tpu_custom_call" | custom-call | tf_op jit(solution)/shard_map/pallas_call | solution.py:558
  156.8 1.3 copy.7
Async XLA Ops:
  0.0 1.6 %copy-start = (f32[32,16384]{1,0:T(8,128)S(1)}, f32[32,16384]{1,0:T(8,128)}, u32[]{:S(2)}) copy-start(f32[32,16384]{1,0:T(8,128)} %c_ref.1) | copy-start | bytes 6291460
  1.6 0.8 copy-start.1
  2.4 0.8 copy-start.2
  3.3 0.7 copy-start.3
  4.0 0.7 copy-start.4

commit v3 on v2

--- a/solution.py
+++ b/solution.py
@@ -15,6 +15,9 @@
 HIGHEST = lax.Precision.HIGHEST
 MESH = pl.DeviceIdType.MESH
 VMEM = pl.BlockSpec(memory_space=pltpu.VMEM)
+FIRST_BATCH = 40
+SECOND_BATCH = 64
+STRIDE = 27
 VMEM_LIMIT = 48 * 1024 * 1024
 
 
@@ -51,24 +54,56 @@
     )
 
 
+PIVOTS = 4
+
+
 def negative_inverse(ref):
-    row_at = lax.broadcasted_iota(jnp.int32, (128, 128), 0)
-    col_at = lax.broadcasted_iota(jnp.int32, (128, 128), 1)
-
-    def step(k, carry):
+    lane = lax.broadcasted_iota(jnp.int32, (1, 128), 1)
+    some = range(PIVOTS)
+
+    def step(h, carry):
+        k = pl.multiple_of(h * PIVOTS, PIVOTS)
+        at = [lane == k + m for m in some]
+        rows = [ref[pl.ds(k + m, 1), :] for m in some]
         a = ref[...]
-        row = ref[pl.ds(k, 1), :]
-        in_col = col_at == k
-        col = jnp.sum(jnp.where(in_col, a, 0.0), axis=1, keepdims=True)
-        pivot = jnp.sum(jnp.where(in_col[0:1], row, 0.0), axis=1, keepdims=True)
-        inv = 1.0 / pivot
-        scaled = row * inv
-        new = a - col * scaled
-        new = jnp.where(in_col, col * inv, new)
-        ref[...] = jnp.where(row_at == k, jnp.where(in_col[0:1], -inv, scaled), new)
-        return carry
-
-    lax.fori_loop(0, 128, step, 0)
+
+        def column(m, of):
+            return jnp.sum(jnp.where(at[m], of, 0.0), axis=1, keepdims=True)
+
+        cols = [column(m, a) for m in some]
+        block = [[column(max(i, j), rows[min(i, j)]) for j in some] for i in some]
+        for m in some:
+            inv = 1.0 / block[m][m]
+            scaled = [block[m][j] * inv for j in some]
+            swept = [[None] * PIVOTS for _ in some]
+            for i in some:
+                for j in range(i, PIVOTS):
+                    if i == m and j == m:
+                        value = -inv
+                    elif i == m:
+                        value = scaled[j]
+                    elif j == m:
+                        value = scaled[i]
+                    else:
+                        value = block[i][j] - block[i][m] * scaled[j]
+                    swept[i][j] = swept[j][i] = value
+            block = swept
+        new = jnp.where((lane >= k) & (lane < k + PIVOTS), 0.0, a)
+        new_rows = []
+        for m in some:
+            row = -block[m][0] * rows[0]
+            for j in range(1, PIVOTS):
+                row = row - block[m][j] * rows[j]
+            for j in some:
+                row = jnp.where(at[j], block[m][j], row)
+            new_rows.append(row)
+            new = new - cols[m] * row
+        ref[...] = new
+        for m in some:
+            ref[pl.ds(k + m, 1), :] = new_rows[m]
+        return carry
+
+    lax.fori_loop(0, 128 // PIVOTS, step, 0)
 
 
 def dot(a, b):
@@ -238,21 +273,22 @@
     def my_columns(c):
         return adv.at[:, pl.ds(pl.multiple_of(r * 512 + lo * 256 + c * 128, 128), 128)]
 
-    def scatter(c):
+    def scatter(c, start, stop):
         def send(i, carry):
-            to = lax.rem(me + i, 2 * MEMBERS)
+            to = lax.rem(me + STRIDE * i, 2 * MEMBERS)
             to_lo, to_r = to // MEMBERS, to % MEMBERS
-            start = pl.multiple_of(to_r * 512 + to_lo * 256 + c * 128, 128)
+            column = pl.multiple_of(to_r * 512 + to_lo * 256 + c * 128, 128)
             remote(
-                adv.at[:, pl.ds(start, 128)], ext.at[c, 16 + me],
+                adv.at[:, pl.ds(column, 128)], ext.at[c, 16 + me],
                 send_sem.at[6 + c], recv_sem.at[7 + c], 2 * y + to_lo, to_r,
             ).start()
             return carry
 
-        lax.fori_loop(1, 2 * MEMBERS, send, 0)
+        lax.fori_loop(start, stop, send, 0)
+
+    for c in range(2):
         pltpu.make_async_copy(my_columns(c), ext.at[c, 16 + me], recv_sem.at[7 + c]).start()
-
-    scatter(0)
+    scatter(0, 1, FIRST_BATCH)
 
     ut = pltpu.roll(u12.T, lax.rem(2 * NX - 16 * y + 2, NX), 1)
     vt = pltpu.roll(v12.T, lax.rem(2 * NX - 16 * y + 2, NX), 1)
@@ -328,13 +364,7 @@
         remote(yt, rt, send_sem.at[4], recv_sem.at[5], chip, 2 * g + core).start()
 
     yg[chip, core] = yt[...]
-
-    def to_group(i, carry):
-        to = lax.rem(r + 2 * i, MEMBERS)
-        remote(yt, yg.at[chip, core], send_sem.at[5], recv_sem.at[6], g, to).start()
-        return carry
-
-    lax.fori_loop(1, GROUPS, to_group, 0)
+    scatter(0, FIRST_BATCH, SECOND_BATCH)
     drain(sparts.at[0:15], recv_sem.at[3])
     srow[...] = jnp.sum(sparts[...], axis=0)
     s_all[r] = srow[...]
@@ -361,7 +391,16 @@
     pltpu.make_async_copy(
         rt.at[:, pl.ds(pl.multiple_of(core * 512, 512), 512)], yr.at[2 * g + core], recv_sem.at[9]
     ).start()
-    scatter(1)
+
+    scatter(0, SECOND_BATCH, 2 * MEMBERS)
+    scatter(1, 1, 2 * MEMBERS)
+
+    def to_group(i, carry):
+        to = lax.rem(r + 2 * i, MEMBERS)
+        remote(yt, yg.at[chip, core], send_sem.at[5], recv_sem.at[6], g, to).start()
+        return carry
+
+    lax.fori_loop(1, GROUPS, to_group, 0)
 
     drain(s_all.at[0:31], recv_sem.at[4])
     diagonal = lax.broadcasted_iota(jnp.int32, (128, 128), 0) == lax.broadcasted_iota(
@@ -371,11 +410,9 @@
     first[...] = 0.5 * (s11 + s11.T) + jnp.where(diagonal, var_ref[0:1, :], 0.0)
     negative_inverse(first)
 
-    drain(yg.at[0:15, 0], recv_sem.at[6])
     relay = remote(
         yg.at[:, core], yg.at[:, core], send_sem.at[9], recv_sem.at[10], g, 2 * chip + 1 - core
     )
-    relay.start()
 
     def up(c):
         return remote(
@@ -412,6 +449,72 @@
     inner = s22 + dot(s21, dot(first[...], s12))
     second[...] = 0.5 * (inner + inner.T) + jnp.where(diagonal, var_ref[1:2, :], 0.0)
     negative_inverse(second)
+    def grid_row(c, k):
+        return jnp.concatenate([ext[c, 4 * k + i] for i in range(4)], axis=0)
+
+    def column_first(c, start, stop):
+        def step(k, carry):
+            q = grid_row(c, k)
+            inside = (y * 16 + k - 4 >= 0) & (y * 16 + k - 4 < NY)
+            slope = column_slope(
+                q, grid_row(c, k + 1), grid_row(c, k - 1), grid_row(c, k + 2), grid_row(c, k - 2),
+                ub[k - 2], vb[k - 2],
+            )
+            mid[k - 2] = jnp.where(inside, q + slope, 0.0)
+            return carry
+
+        lax.fori_loop(start, stop, step, 0)
+
+    def column_second(c, half):
+        def step(j, carry):
+            k = half * 8 + j + 4
+            q = mid[k - 2]
+            slope = column_slope(
+                q, mid[k - 1], mid[k - 3], mid[k], mid[k - 4], ub[k - 2], vb[k - 2]
+            )
+            fore[c, half, j] = 0.5 * (grid_row(c, k) + q + slope)
+            return carry
+
+        lax.fori_loop(0, 8, step, 0)
+
+    def correct(column, field):
+        cols = pl.ds(pl.multiple_of(column, 128), 128)
+        b_high, b_low = zh[:, cols], zl[:, cols]
+
+        def part(a, b):
+            return jnp.dot(a, b, preferred_element_type=f32)
+
+        def step(j, carry):
+            a_high, a_low = qh[j], ql[j]
+            out_ref[pl.ds(pl.multiple_of(j * NX, NX), NX), cols] = field(j) - (
+                part(a_high, b_high) + part(a_high, b_low) + part(a_low, b_high)
+            )
+            return carry
+
+        lax.fori_loop(0, 8, step, 0)
+
+    for c in range(2):
+        if c == 1:
+            start_halo(1)
+        column_first(c, 6, 18)
+        if c == 1:
+            drain(yg.at[0:15, 0], recv_sem.at[6])
+            relay.start()
+
+        @pl.when(y > 0)
+        def _():
+            up(c).wait_recv()
+
+        @pl.when(y < 7)
+        def _():
+            down(c).wait_recv()
+
+        column_first(c, 2, 6)
+        column_first(c, 18, 22)
+        column_second(c, 1 - lo)
+        trade(c).start()
+        column_second(c, lo)
+
     drain(yr, recv_sem.at[9])
     r1 = yr[0:16].reshape(128, 512)
     r2 = yr[16:32].reshape(128, 512)
@@ -427,69 +530,7 @@
         high = q.astype(bf16)
         qh[j] = high
         ql[j] = (q - high.astype(f32)).astype(bf16)
-
-    def grid_row(c, k):
-        return jnp.concatenate([ext[c, 4 * k + i] for i in range(4)], axis=0)
-
-    def column_first(c, start, stop):
-        def step(k, carry):
-            q = grid_row(c, k)
-            inside = (y * 16 + k - 4 >= 0) & (y * 16 + k - 4 < NY)
-            slope = column_slope(
-                q, grid_row(c, k + 1), grid_row(c, k - 1), grid_row(c, k + 2), grid_row(c, k - 2),
-                ub[k - 2], vb[k - 2],
-            )
-            mid[k - 2] = jnp.where(inside, q + slope, 0.0)
-            return carry
-
-        lax.fori_loop(start, stop, step, 0)
-
-    def column_second(c, half):
-        def step(j, carry):
-            k = half * 8 + j + 4
-            q = mid[k - 2]
-            slope = column_slope(
-                q, mid[k - 1], mid[k - 3], mid[k], mid[k - 4], ub[k - 2], vb[k - 2]
-            )
-            fore[c, half, j] = 0.5 * (grid_row(c, k) + q + slope)
-            return carry
-
-        lax.fori_loop(0, 8, step, 0)
-
-    def correct(column, field):
-        cols = pl.ds(pl.multiple_of(column, 128), 128)
-        b_high, b_low = zh[:, cols], zl[:, cols]
-
-        def part(a, b):
-            return jnp.dot(a, b, preferred_element_type=f32)
-
-        def step(j, carry):
-            a_high, a_low = qh[j], ql[j]
-            out_ref[pl.ds(pl.multiple_of(j * NX, NX), NX), cols] = field(j) - (
-                part(a_high, b_high) + part(a_high, b_low) + part(a_low, b_high)
-            )
-            return carry
-
-        lax.fori_loop(0, 8, step, 0)
-
     for c in range(2):
-        if c == 1:
-            start_halo(1)
-        column_first(c, 6, 18)
-
-        @pl.when(y > 0)
-        def _():
-            up(c).wait_recv()
-
-        @pl.when(y < 7)
-        def _():
-            down(c).wait_recv()
-
-        column_first(c, 2, 6)
-        column_first(c, 18, 22)
-        column_second(c, 1 - lo)
-        trade(c).start()
-        column_second(c, lo)
         correct(lo * 256 + c * 128, lambda j: fore[c, lo, j])
     for c in range(2):
         trade(c).wait_recv()

time: 158 us -> 132 us (0.84)
  the two profiles are of different devices: /device:TPU:30 before, /device:TPU:112 now
where the time goes in v3:
time: 132 us
  Pallas kernels  126 us (95%)
  local copies, waits for them, and re-layouts  5.95 us (5%)
    pallas_call x1, Pallas kernels, local(): pl.pallas_call(kernel, out_shape=jax.ShapeDtypeStruct((1024, 512), f32),...  126 us
    unnamed x11, local copies, waits for them, and re-layouts  5.95 us

profile of v3, /device:TPU:112, one launch (start us, length us, event | category | flops | bytes accessed | tf_op | source)
XLA Modules:
  0.0 131.8 jit_solution(8237728369876711545)
XLA Ops:
  0.0 0.0 copy-start
  0.0 1.6 %copy-done = f32[32,16384]{1,0:T(8,128)S(1)} copy-done((f32[32,16384]{1,0:T(8,128)S(1)}, f32[32,16384]{1,0:T(8,128)}, u32[]{:S(2)}) %copy-start) | copy-done | bytes 2097176
  1.6 0.0 copy-start.1
  1.6 0.8 copy-done.1
  2.4 0.0 copy-start.2
  2.4 0.8 copy-done.2
  3.3 0.0 copy-start.3
  3.3 0.7 copy-done.3
  4.0 0.0 copy-start.4
  4.0 0.7 copy-done.4
  4.6 125.8 %shard_map.55 = f32[1024,512]{1,0:T(8,128)S(1)} custom-call(s32[1,256]{1,0:T(1,128)S(1)} %bitcast.1, f32[32,16384]{1,0:T(8,128)S(1)} %copy-done, f32[128,128]{1,0:T(8,128)S(1)} %copy-done.1, f32[128,128]{1,0:T(8,128)S(1)} %copy-done.2, f32[2,128]{1,0:T(2,128)S(1)} %copy-done.4), custom_call_target="tpu_custom_call" | custom-call | tf_op jit(solution)/shard_map/pallas_call | solution.py:599
  130.5 1.3 %copy.7 = f32[1024,512]{1,0:T(8,128)} copy(f32[1024,512]{1,0:T(8,128)S(1)} %shard_map.55) | data formatting | bytes 4194304
Async XLA Ops:
  0.0 1.6 %copy-start = (f32[32,16384]{1,0:T(8,128)S(1)}, f32[32,16384]{1,0:T(8,128)}, u32[]{:S(2)}) copy-start(f32[32,16384]{1,0:T(8,128)} %c_ref.1) | copy-start | bytes 6291460
  1.6 0.8 copy-start.1
  2.4 0.8 copy-start.2
  3.3 0.7 copy-start.3
  4.0 0.7 copy-start.4

commit v4 on v3

--- a/solution.py
+++ b/solution.py
@@ -17,8 +17,9 @@
 VMEM = pl.BlockSpec(memory_space=pltpu.VMEM)
 FIRST_BATCH = 40
 SECOND_BATCH = 64
+EARLY = 1
 STRIDE = 27
-VMEM_LIMIT = 48 * 1024 * 1024
+VMEM_LIMIT = 62 * 1024 * 1024
 
 
 def lane_slope(cf, q, yp1, ym1, yp2, ym2):
@@ -127,9 +128,9 @@
 
 
 def kernel(
-    obs_row_ref, c_ref, u_ref, v_ref, var_ref, out_ref,
-    coef, q1, adv, aot, pieces, near, mid8, yt, rt, spart, sparts, srow, s_all, yg, yr, first, second,
-    ext, mid, fore, theirs, ub, vb, qh, ql, zh, zl, send_sem, recv_sem,
+    obs_in, c_in, u_in, v_in, var_in, out_ref,
+    obs_row_ref, c_ref, u_ref, v_ref, var_ref, coef, q1, adv, aot, pieces, near, mid8, yt, rt, spart, sparts, srow, s_all, yg, yr, first, second,
+    ext, mid, fore, theirs, ub, vb, qh, ql, zh, zl, chosen, send_sem, recv_sem, load_sem,
 ):
     f32, bf16 = jnp.float32, jnp.bfloat16
     g = lax.axis_index("grp")
@@ -138,6 +139,15 @@
     chip, core = r // 2, r % 2
     me = lo * MEMBERS + r
 
+    loads = [
+        pltpu.make_async_copy(source, target, load_sem.at[k])
+        for k, (source, target) in enumerate(
+            ((u_in, u_ref), (v_in, v_ref), (obs_in, obs_row_ref), (c_in, c_ref), (var_in, var_ref))
+        )
+    ]
+    for load in loads:
+        load.start()
+
     barrier = pltpu.get_barrier_semaphore()
 
     def greet(grp, row):
@@ -172,6 +182,9 @@
     @pl.when(jnp.logical_not(on_diagonal))
     def _():
         greet(chip, 2 * g + core)
+
+    for load in loads:
+        load.wait()
 
     gx = lax.broadcasted_iota(jnp.int32, (NY, NX), 1)
     gy = lax.broadcasted_iota(jnp.int32, (NY, NX), 0)
@@ -210,7 +223,7 @@
 
     cells = obs_row_ref[...]
     chosen_x = jnp.where(
-        lax.broadcasted_iota(jnp.int32, (NX, OBS), 0) == cells % NX, 1.0, 0.0
+        lax.broadcasted_iota(jnp.int32, (2 * NX, OBS), 0) % NX == cells % NX, 1.0, 0.0
     ).astype(bf16)
     cells_y = cells // NX
 
@@ -218,13 +231,10 @@
         new = 0.5 * (c_ref[:, lanes(yy)] + q1[:, lanes(yy)] + row_slope(q1, yy))
         adv[:, lanes(yy)] = new
         high = new.astype(bf16)
-        rest = new - high.astype(f32)
-        middle = rest.astype(bf16)
-        low = (rest - middle.astype(f32)).astype(bf16)
-        parts = jnp.dot(
-            jnp.concatenate([high, middle, low], axis=0), chosen_x, preferred_element_type=f32
+        low = (new - high.astype(f32)).astype(bf16)
+        found = jnp.dot(
+            jnp.concatenate([high, low], axis=1), chosen_x, preferred_element_type=f32
         )
-        found = parts[0:ROWS] + (parts[ROWS : 2 * ROWS] + parts[2 * ROWS :])
         return jnp.where(cells_y == yy, found, acc)
 
     lax.fori_loop(0, NY, row_first, 0, unroll=4)
@@ -273,6 +283,10 @@
     def my_columns(c):
         return adv.at[:, pl.ds(pl.multiple_of(r * 512 + lo * 256 + c * 128, 128), 128)]
 
+    def arrival(c, source):
+        outer = jnp.where(source < 16, source, source - 32)
+        return jnp.where((source >= 16) & (source < 48), 7 + c, 17 + 32 * c + outer)
+
     def scatter(c, start, stop):
         def send(i, carry):
             to = lax.rem(me + STRIDE * i, 2 * MEMBERS)
@@ -280,14 +294,14 @@
             column = pl.multiple_of(to_r * 512 + to_lo * 256 + c * 128, 128)
             remote(
                 adv.at[:, pl.ds(column, 128)], ext.at[c, 16 + me],
-                send_sem.at[6 + c], recv_sem.at[7 + c], 2 * y + to_lo, to_r,
+                send_sem.at[6 + c], recv_sem.at[arrival(c, me)], 2 * y + to_lo, to_r,
             ).start()
             return carry
 
         lax.fori_loop(start, stop, send, 0)
 
     for c in range(2):
-        pltpu.make_async_copy(my_columns(c), ext.at[c, 16 + me], recv_sem.at[7 + c]).start()
+        pltpu.make_async_copy(my_columns(c), ext.at[c, 16 + me], recv_sem.at[arrival(c, me)]).start()
     scatter(0, 1, FIRST_BATCH)
 
     ut = pltpu.roll(u12.T, lax.rem(2 * NX - 16 * y + 2, NX), 1)
@@ -314,6 +328,9 @@
         for c in range(2):
             ext[c, 80:96] = jnp.zeros((16, ROWS, NX), f32)
 
+    cell_at = lax.broadcasted_iota(jnp.int32, (1024, OBS), 0)
+    chosen[...] = jnp.where(cell_at == obs_row_ref[...] - 1024 * g, 1.0, 0.0).astype(bf16)
+
     drain(pieces.at[16:48], recv_sem.at[0])
 
     @pl.when(g > 0)
@@ -343,9 +360,14 @@
     for k in range(4, 12):
         yt[:, (k - 4) * NX : (k - 3) * NX] = 0.5 * (at(near, k) + at(mid8, k) + near_slope(mid8, k))
 
-    cell_at = lax.broadcasted_iota(jnp.int32, (1024, OBS), 0)
-    chosen = jnp.where(cell_at == obs_row_ref[...] - 1024 * g, 1.0, 0.0)
-    spart[...] = dot(yt[...], chosen)
+    whole = yt[...]
+    high = whole.astype(bf16).astype(f32)
+    middle = (whole - high).astype(bf16).astype(f32)
+    stacked = jnp.concatenate(
+        [high, middle, whole - high - middle, jnp.zeros((8, 1024), f32)], axis=0
+    ).astype(bf16)
+    parts = jnp.dot(stacked, chosen[...], preferred_element_type=f32)
+    spart[...] = parts[0:8] + (parts[8:16] + parts[16:24])
     sparts[g] = spart[...]
 
     def to_groups(i, carry):
@@ -365,6 +387,7 @@
 
     yg[chip, core] = yt[...]
     scatter(0, FIRST_BATCH, SECOND_BATCH)
+    scatter(1, 1, EARLY)
     drain(sparts.at[0:15], recv_sem.at[3])
     srow[...] = jnp.sum(sparts[...], axis=0)
     s_all[r] = srow[...]
@@ -393,7 +416,7 @@
     ).start()
 
     scatter(0, SECOND_BATCH, 2 * MEMBERS)
-    scatter(1, 1, 2 * MEMBERS)
+    scatter(1, EARLY, 2 * MEMBERS)
 
     def to_group(i, carry):
         to = lax.rem(r + 2 * i, MEMBERS)
@@ -414,34 +437,38 @@
         yg.at[:, core], yg.at[:, core], send_sem.at[9], recv_sem.at[10], g, 2 * chip + 1 - core
     )
 
-    def up(c):
-        return remote(
-            ext.at[c, 64:80], ext.at[c, 0:16], send_sem.at[10 + c], recv_sem.at[11 + c], g + 2, r
-        )
-
-    def down(c):
-        return remote(
-            ext.at[c, 16:32], ext.at[c, 80:96], send_sem.at[12 + c], recv_sem.at[13 + c], g - 2, r
-        )
-
     def trade(c):
         return remote(
             fore.at[c, 1 - lo], theirs.at[c], send_sem.at[14 + c], recv_sem.at[15 + c],
             2 * y + 1 - lo, r,
         )
 
-    def start_halo(c):
-        drain(ext.at[c, 16:80], recv_sem.at[7 + c])
-
-        @pl.when(y < 7)
-        def _():
-            up(c).start()
-
-        @pl.when(y > 0)
-        def _():
-            down(c).start()
-
-    start_halo(0)
+    def forward(c, start, stop):
+        def step(i, carry):
+            source = lax.rem(me + (2 * MEMBERS - STRIDE) * i, 2 * MEMBERS)
+            block = ext.at[c, 16 + source]
+
+            @pl.when((source < 16) | (source >= 48))
+            def _():
+                drain(block, recv_sem.at[arrival(c, source)])
+
+            @pl.when((source < 16) & (y > 0))
+            def _():
+                remote(
+                    block, ext.at[c, 80 + source], send_sem.at[12 + c], recv_sem.at[13 + c], g - 2, r
+                ).start()
+
+            @pl.when((source >= 48) & (y < 7))
+            def _():
+                remote(
+                    block, ext.at[c, source - 48], send_sem.at[10 + c], recv_sem.at[11 + c], g + 2, r
+                ).start()
+
+            return carry
+
+        lax.fori_loop(start, stop, step, 0)
+
+    forward(0, 0, 2 * MEMBERS)
 
     s12 = s_all[0:16, :, 128:256].reshape(128, 128)
     s21 = s_all[16:32, :, 0:128].reshape(128, 128)
@@ -478,36 +505,40 @@
         lax.fori_loop(0, 8, step, 0)
 
     def correct(column, field):
-        cols = pl.ds(pl.multiple_of(column, 128), 128)
+        cols = pl.ds(pl.multiple_of(column, 256), 256)
         b_high, b_low = zh[:, cols], zl[:, cols]
 
         def part(a, b):
             return jnp.dot(a, b, preferred_element_type=f32)
 
-        def step(j, carry):
-            a_high, a_low = qh[j], ql[j]
-            out_ref[pl.ds(pl.multiple_of(j * NX, NX), NX), cols] = field(j) - (
-                part(a_high, b_high) + part(a_high, b_low) + part(a_low, b_high)
-            )
-            return carry
-
-        lax.fori_loop(0, 8, step, 0)
-
+        def step(i, carry):
+            rows = pl.ds(pl.multiple_of(i * 256, 256), 256)
+            a_high, a_low = qh[rows, :], ql[rows, :]
+            product = part(a_high, b_high) + (part(a_high, b_low) + part(a_low, b_high))
+            for c in range(2):
+                for k in range(2):
+                    j = 2 * i + k
+                    place = pl.ds(pl.multiple_of(column + c * 128, 128), 128)
+                    out_ref[pl.ds(pl.multiple_of(j * NX, NX), NX), place] = (
+                        field(c, j) - product[k * 128 : (k + 1) * 128, c * 128 : (c + 1) * 128]
+                    )
+            return carry
+
+        lax.fori_loop(0, 4, step, 0)
+
+    forward(1, 0, 32)
     for c in range(2):
         if c == 1:
-            start_halo(1)
+            forward(1, 32, 2 * MEMBERS)
+        drain(ext.at[c, 32:64], recv_sem.at[7 + c])
         column_first(c, 6, 18)
-        if c == 1:
-            drain(yg.at[0:15, 0], recv_sem.at[6])
-            relay.start()
-
         @pl.when(y > 0)
         def _():
-            up(c).wait_recv()
+            drain(ext.at[c, 0:16], recv_sem.at[11 + c])
 
         @pl.when(y < 7)
         def _():
-            down(c).wait_recv()
+            drain(ext.at[c, 80:96], recv_sem.at[13 + c])
 
         column_first(c, 2, 6)
         column_first(c, 18, 22)
@@ -515,6 +546,8 @@
         trade(c).start()
         column_second(c, lo)
 
+    drain(yg.at[0:15, 0], recv_sem.at[6])
+    relay.start()
     drain(yr, recv_sem.at[9])
     r1 = yr[0:16].reshape(128, 512)
     r2 = yr[16:32].reshape(128, 512)
@@ -528,13 +561,20 @@
     for j in range(8):
         q = yg[:, :, :, j * NX : (j + 1) * NX].reshape(OBS, NX).T
         high = q.astype(bf16)
-        qh[j] = high
-        ql[j] = (q - high.astype(f32)).astype(bf16)
-    for c in range(2):
-        correct(lo * 256 + c * 128, lambda j: fore[c, lo, j])
+        qh[j * NX : (j + 1) * NX] = high
+        ql[j * NX : (j + 1) * NX] = (q - high.astype(f32)).astype(bf16)
+    correct(lo * 256, lambda c, j: fore[c, lo, j])
+    correct((1 - lo) * 256, lambda c, j: 0.0)
     for c in range(2):
         trade(c).wait_recv()
-        correct((1 - lo) * 256 + c * 128, lambda j: theirs[c, j])
+
+        def finish(j, carry):
+            rows = pl.ds(pl.multiple_of(j * NX, NX), NX)
+            place = pl.ds(pl.multiple_of((1 - lo) * 256 + c * 128, 128), 128)
+            out_ref[rows, place] = out_ref[rows, place] + theirs[c, j]
+            return carry
+
+        lax.fori_loop(0, 8, finish, 0)
 
     drain(pieces.at[0:31], send_sem.at[0])
 
@@ -558,16 +598,21 @@
 
         @pl.when(y < 7)
         def _():
-            up(c).wait_send()
+            drain(ext.at[c, 0:16], send_sem.at[10 + c])
 
         @pl.when(y > 0)
         def _():
-            down(c).wait_send()
+            drain(ext.at[c, 80:96], send_sem.at[12 + c])
 
 
 def local(cov_prior, courant_x_field, courant_y_field, obs_cells, obs_var):
     f32, bf16 = jnp.float32, jnp.bfloat16
     scratch = [
+        ((1, OBS), jnp.int32),
+        ((ROWS, NCELL), f32),
+        ((NY, NX), f32),
+        ((NY, NX), f32),
+        ((2, NX), f32),
         ((8, 136, NX), f32),
         ((ROWS, NCELL), f32),
         ((ROWS, NCELL), f32),
@@ -591,18 +636,19 @@
         ((2, 8, NX, NX), f32),
         ((20, NX, NX), f32),
         ((20, NX, NX), f32),
-        ((8, NX, OBS), bf16),
-        ((8, NX, OBS), bf16),
+        ((1024, OBS), bf16),
+        ((1024, OBS), bf16),
         ((OBS, 512), bf16),
         ((OBS, 512), bf16),
+        ((1024, OBS), bf16),
     ]
     return pl.pallas_call(
         kernel,
         out_shape=jax.ShapeDtypeStruct((1024, 512), f32),
-        in_specs=[VMEM] * 5,
+        in_specs=[pl.BlockSpec(memory_space=pltpu.HBM)] * 5,
         out_specs=VMEM,
         scratch_shapes=[pltpu.VMEM(shape, dtype) for shape, dtype in scratch]
-        + [pltpu.SemaphoreType.DMA((16,)), pltpu.SemaphoreType.DMA((17,))],
+        + [pltpu.SemaphoreType.DMA((16,)), pltpu.SemaphoreType.DMA((81,)), pltpu.SemaphoreType.DMA((5,))],
         compiler_params=pltpu.CompilerParams(
             collective_id=0, has_side_effects=True, vmem_limit_bytes=VMEM_LIMIT
         ),

time: 132 us -> 129 us (0.977)
  local copies, waits for them, and re-layouts: 5.95 us -> 3.08 us
    unnamed x11 -> x1, local copies, waits for them, and re-layouts: 5.95 us -> 3.08 us
where the time goes in v4:
time: 129 us; the launch traced here: 128 us
  Pallas kernels  125 us (97%)
  local copies, waits for them, and re-layouts  3.08 us (2%)
    pallas_call x1, Pallas kernels, local(): pl.pallas_call(kernel, out_shape=jax.ShapeDtypeStruct((1024, 512), f32),...  125 us
    unnamed x1, local copies, waits for them, and re-layouts  3.08 us

profile of v4, /device:TPU:112, one launch (start us, length us, event | category | flops | bytes accessed | tf_op | source)
XLA Modules:
  0.0 128.2 jit_solution(4132691157502932954)
XLA Ops:
  0.0 125.1 %shard_map.55 = f32[1024,512]{1,0:T(8,128)} custom-call(s32[1,256]{1,0:T(1,128)} %bitcast.1, f32[32,16384]{1,0:T(8,128)} %c_in.1, f32[128,128]{1,0:T(8,128)} %u_in.1, f32[128,128]{1,0:T(8,128)} %v_in.1, f32[2,128]{1,0:T(2,128)} %var_in.1), custom_call_target="tpu_custom_call" | custom-call | tf_op jit(solution)/shard_map/pallas_call | solution.py:645
  125.1 3.1 %copy.7 = f32[1024,512]{1,0:T(8,128)} copy(f32[1024,512]{1,0:T(8,128)} %shard_map.55) | data formatting | bytes 4194304
